TPU v7x, 512 devices: a whole 4x4x16 slice. The times are simulated.
512 devices in a mesh: dp: 4 (over z_lo), context: 16 (over x, z_hi), tensor: 8 (over y, core).
Axes of the slice: x: 4, y: 4, z: 16 (z_hi: 4, z_lo: 4; z = z_hi * 4 + z_lo), core: 2. Of those that a mesh axis runs over, the one named last changes fastest.
Arguments:
- queries: bfloat16 [4, 3072, 5120], P('dp', 'context', 'tensor'), may hold values from -80 to 80
- keys: bfloat16 [4, 3072, 1024], P('dp', 'context', 'tensor'), may hold values from -5 to 5
- memory: bfloat16 [4, 3072, 5120], P('dp', 'context'), may hold values from -6 to 6
- value_weight: bfloat16 [5120, 1024], P(None, 'tensor'), may hold values from -0.078125 to 0.078125
- doc_ids: int32 [4, 3072], P('dp'), may hold values from 0 to 7, never falling along the last dimension, each value on 1 to 1536 neighbouring positions
- out_grad: bfloat16 [4, 3072, 5120], P('dp', 'context', 'tensor'), may hold values from -6 to 6
Outputs:
- attended: bfloat16 [4, 3072, 5120], P('dp', 'context', 'tensor')
- grad_queries: bfloat16 [4, 3072, 5120], P('dp', 'context', 'tensor')
- grad_keys: bfloat16 [4, 3072, 1024], P('dp', 'context', 'tensor')
- grad_value_weight: float32 [5120, 1024], P(('dp', 'context'), 'tensor')
Inputs may be any that keep to these rules, and one draw needn't show every extreme that they name: `doc_ids`: document numbers never fall along a sequence and every number appears; one document holds exactly 1536 positions.
All inputs are finite; a program needn't handle non-finite values.
Results may differ from a plain program's by a relative error of at most 0.015.
Values may be sent and summed in bfloat16 or wider, within the bound.
A program may use at most 128 MiB of HBM per device.

v0:
```python
import jax
import jax.numpy as jnp
from jax import lax
from jax.sharding import PartitionSpec as P

HD = 128


NEG_FILL = -1e30


def raw_products(left_side, right_side):
    return jnp.einsum("qgjd,kgd->qgjk", left_side, right_side, preferred_element_type=jnp.float32)


def on_device(queries, keys, memory, value_weight, doc_ids, out_grad):
    tok_rows = queries.shape[1]
    kv_local = keys.shape[2] // HD
    group_size = queries.shape[2] // keys.shape[2]
    query_heads = queries[0].reshape(tok_rows, kv_local, group_size, HD)
    out_heads = out_grad[0].reshape(tok_rows, kv_local, group_size, HD)
    memory_rows = memory[0]
    values = jnp.dot(memory_rows, value_weight, preferred_element_type=jnp.float32).astype(
        jnp.bfloat16
    )
    doc_row = doc_ids[0]
    offset = lax.axis_index("context") * tok_rows
    key_flat, value_flat = (
        lax.all_gather(keys[0], "context", axis=0, tiled=True),
        lax.all_gather(values, "context", axis=0, tiled=True),
    )
    key_count = key_flat.shape[0]
    key_pos = jnp.arange(key_count, dtype=jnp.int32)
    key_all = key_flat.reshape(key_count, kv_local, HD)
    value_all = value_flat.reshape(key_count, kv_local, HD)
    query_pos = offset + jnp.arange(tok_rows, dtype=jnp.int32)
    query_docs = lax.dynamic_slice_in_dim(doc_row, offset, tok_rows, 0)
    visible = (query_docs[:, None] == doc_row[None, :]) & (key_pos[None, :] <= query_pos[:, None])
    visible_heads = visible[:, None, None, :]
    score_scale = HD ** (-0.5)
    scores = raw_products(query_heads, key_all) * score_scale
    scores = jnp.where(visible_heads, scores, NEG_FILL)
    row_top = jnp.max(scores, axis=-1, keepdims=True)
    exp_rows = jnp.exp(scores - row_top)
    softmax_rows = exp_rows / jnp.sum(exp_rows, axis=-1, keepdims=True)
    probs_half = softmax_rows.astype(jnp.bfloat16)
    attended = jnp.einsum(
        "qgjk,kgd->qgjd", probs_half, value_all, preferred_element_type=jnp.float32
    ).astype(jnp.bfloat16)
    grad_probs = raw_products(out_heads, value_all)
    row_delta = jnp.sum(
        out_heads.astype(jnp.float32) * attended.astype(jnp.float32), axis=-1, keepdims=True
    )
    grad_scores = (softmax_rows * (grad_probs - row_delta) * score_scale).astype(jnp.bfloat16)
    grad_query = jnp.einsum(
        "qgjk,kgd->qgjd", grad_scores, key_all, preferred_element_type=jnp.float32
    ).astype(jnp.bfloat16)
    key_part = jnp.einsum(
        "qgjk,qgjd->kgd", grad_scores, query_heads, preferred_element_type=jnp.float32
    )
    value_part = jnp.einsum(
        "qgjk,qgjd->kgd", probs_half, out_heads, preferred_element_type=jnp.float32
    )
    key_part = key_part.reshape(key_count, kv_local * HD)
    value_part = value_part.reshape(key_count, kv_local * HD)
    key_sum, value_sum = (
        lax.psum_scatter(
            key_part.astype(jnp.bfloat16), "context", scatter_dimension=0, tiled=True
        ).astype(jnp.float32),
        lax.psum_scatter(
            value_part.astype(jnp.bfloat16), "context", scatter_dimension=0, tiled=True
        ).astype(jnp.float32),
    )
    grad_values = value_sum.astype(jnp.bfloat16)
    weight_grad = lax.psum_scatter(
        lax.dot_general(
            memory_rows, grad_values, (((0,), (0,)), ((), ())), preferred_element_type=jnp.float32
        ),
        ("dp", "context"),
        scatter_dimension=0,
        tiled=True,
    )
    attended_out = attended.reshape(1, tok_rows, kv_local * group_size * HD)
    query_out = grad_query.reshape(1, tok_rows, kv_local * group_size * HD)
    key_out = key_sum.astype(jnp.bfloat16)[None]
    return (attended_out, query_out, key_out, weight_grad)


def solution(mesh):
    in_specs = (
        P("dp", "context", "tensor"),
        P("dp", "context", "tensor"),
        P("dp", "context", None),
        P(None, "tensor"),
        P("dp", None),
        P("dp", "context", "tensor"),
    )
    out_specs = (
        P("dp", "context", "tensor"),
        P("dp", "context", "tensor"),
        P("dp", "context", "tensor"),
        P(("dp", "context"), "tensor"),
    )
    return jax.shard_map(
        on_device, mesh=mesh, in_specs=in_specs, out_specs=out_specs, check_vma=False
    )
```

profile of v0, /device:TPU:56, one launch (start us, length us, event | category | flops | bytes accessed | tf_op | source)
XLA Modules:
  0.0 752.5 jit_solution(12811126616650463332)
XLA Ops:
  7.2 0.0 copy-start
  7.2 0.0 reduce-scatter.8.cloned.1.call-start
  7.2 2.0 copy.26
  9.2 66.6 %all-gather = bf16[1,3072,128]{2,1,0:T(8,128)(2,1)S(1)} all-gather(bf16[1,192,128]{2,1,0:T(8,128)(2,1)} %param.7), channel_id=2, replica_groups=mesh['dp'=4,'context'=16,'tensor'=8] {'context'}, dimensions={1}, use_global_device_ids=true | all-gather | bytes 835584 | tf_op jit(solution)/shard_map/all_gather | solution.py:29
  75.7 1.8 copy.29
  77.6 0.8 constant_dynamic-slice_fusion
  78.3 1.2 fusion.26
  79.6 0.0 copy-start.3
  79.6 3.3 fusion.4
  82.9 0.0 copy-start.1
  83.0 3.1 fusion.3
  86.1 1.3 copy-done.1
  87.3 0.0 copy-done.3
  87.3 5.5 fusion.23
  92.9 0.0 reduce-scatter.8.cloned.1.call-update
  92.9 0.0 reduce-scatter.6.cloned.1.call-start
  92.9 2.0 copy.31
  94.9 2.1 copy.32
  97.0 0.0 copy-done
  97.0 2.0 fusion.42
  99.0 0.0 slice-start
  99.0 61.6 %all_gather.6 = bf16[3072,128]{1,0:T(8,128)(2,1)S(1)} all-gather(bf16[192,128]{1,0:T(8,128)(2,1)S(1)} %fusion.42), channel_id=1, replica_groups=mesh['dp'=4,'context'=16,'tensor'=8] {'context'}, dimensions={0}, use_global_device_ids=true | all-gather | bytes 835584 | tf_op jit(solution)/shard_map/all_gather | solution.py:30
  160.7 0.0 slice-start.1
  160.7 8.2 %multiply_reduce_fusion = (f32[192,5]{0,1:T(8,128)S(1)}, bf16[192,1,5,128]{3,0,2,1:T(8,128)(2,1)}) fusion(f32[192,1,5,128]{3,0,2,1:T(8,128)} %copy.32, f32[192,5]{0,1:T(8,128)S(1)} %fusion.3, f32[192,5]{0,1:T(8,128)S(1)} %get-tuple-element.16, f32[3072,192,5]{0,1,2:T(8,128)} %copy-done.1, pred[192,3072]{1,0:T(8,128)(4,1)S(1)} %fusion.26, ...), kind=kOutput, calls=%fused_computation.38 | convolution fusion | flops 770210880 | bytes 13921536 | tf_op jit(solution)/shard_map/qgjk,kgd->qgjd/dot_general | solution.py:47
  168.9 0.0 slice-done
  168.9 0.0 slice-done.1
  168.9 0.0 slice-done.2
  168.9 0.0 copy-done.4
  168.9 0.0 copy-start.2
  168.9 5.4 fusion.1
  174.4 0.0 copy-start.6
  174.4 2.5 copy-done.6
  176.9 0.0 copy-done.2
  176.9 3.3 fusion.20
  180.2 0.0 reduce-scatter.6.cloned.1.call-update
  180.2 0.0 reduce-scatter.10.cloned.1.call-start
  180.3 42.6 %reduce-scatter.8.cloned.1.call-done = bf16[192,128]{1,0:T(8,128)(2,1)} async-done(((bf16[3072,128]{1,0:T(8,128)(2,1)}), bf16[192,128]{1,0:T(8,128)(2,1)}) %reduce-scatter.8.cloned.1.call-update) | async-done | bytes 49168 | tf_op jit(solution)/shard_map/reduce_scatter | solution.py:70
  222.9 2.9 convolution_bitcast_fusion
  225.8 3.2 copy.43
  229.0 0.0 reduce-scatter.10.cloned.1.call-update
  229.1 0.0 copy-done.5
  229.1 0.2 copy.28
  229.3 0.9 copy.36
  230.1 4.3 fusion.36
  234.5 0.2 copy.33
  234.6 0.9 copy.37
  235.5 99.1 %reduce-scatter.6.cloned.1.call-done = bf16[192,128]{1,0:T(8,128)(2,1)} async-done(((bf16[3072,128]{1,0:T(8,128)(2,1)}), bf16[192,128]{1,0:T(8,128)(2,1)}) %reduce-scatter.6.cloned.1.call-update) | async-done | bytes 49168 | tf_op jit(solution)/shard_map/reduce_scatter | solution.py:67
  334.6 411.4 %reduce-scatter.10.cloned.1.call-done = f32[80,128]{1,0:T(8,128)} async-done(((f32[5120,128]{1,0:T(8,128)}), f32[80,128]{1,0:T(8,128)}) %reduce-scatter.10.cloned.1.call-update) | async-done | bytes 40976
  (5 shorter events, 0.0 us)
Async XLA Ops:
  7.2 89.9 %copy-start = (bf16[1,192,5120]{2,1,0:T(8,128)(2,1)S(1)}, bf16[1,192,5120]{2,1,0:T(8,128)(2,1)}, u32[]{:S(2)}) copy-start(bf16[1,192,5120]{2,1,0:T(8,128)(2,1)} %param.8) | copy-start | bytes 5898244
  7.2 215.7 %reduce-scatter.8.cloned.1.call-start = ((), (), s32[]{:S(2)}) async-start(), calls=%async_computation.4 | async-start | bytes 835584 | tf_op jit(solution)/shard_map/reduce_scatter | solution.py:70
  79.6 7.8 %copy-start.3 = (bf16[1,192,640]{1,2,0:T(8,128)(2,1)S(1)}, bf16[1,192,640]{1,2,0:T(8,128)(2,1)}, u32[]{:S(2)}) copy-start(bf16[1,192,640]{1,2,0:T(8,128)(2,1)} %copy.29) | copy-start | bytes 737284
  82.9 4.4 copy-start.1
  92.9 241.7 %reduce-scatter.6.cloned.1.call-start = ((), (), s32[]{:S(2)}) async-start(), calls=%async_computation.3 | async-start | bytes 835584 | tf_op jit(solution)/shard_map/reduce_scatter | solution.py:67
  99.0 69.9 %slice-start = ((s8[11796480]{0:T(1024)(128)(4,1)}), s8[4194304]{0:T(1024)(128)(4,1)S(1)}, s32[]{:S(2)}) async-start(s8[11796480]{0:T(1024)(128)(4,1)} %bitcast.117), calls=%async_computation.6 | async-start | bytes 8388608
  160.7 8.2 %slice-start.1 = ((s8[11796480]{0:T(1024)(128)(4,1)}), s8[4194304]{0:T(1024)(128)(4,1)S(1)}, s32[]{:S(2)}) async-start(s8[11796480]{0:T(1024)(128)(4,1)} %bitcast.117), calls=%async_computation.7 | async-start | bytes 8388608
  160.7 8.2 %slice-start.2 = ((s8[11796480]{0:T(1024)(128)(4,1)}), s8[3407872]{0:T(1024)(128)(4,1)S(1)}, s32[]{:S(2)}) async-start(s8[11796480]{0:T(1024)(128)(4,1)} %bitcast.117), calls=%async_computation.8 | async-start | bytes 6815744
  160.7 8.3 %copy-start.4 = (bf16[1,192,640]{1,2,0:T(8,128)(2,1)S(1)}, bf16[1,192,640]{1,2,0:T(8,128)(2,1)}, u32[]{:S(2)}) copy-start(bf16[1,192,640]{1,2,0:T(8,128)(2,1)} %copy.29) | copy-start | bytes 737284
  168.9 8.0 %copy-start.2 = (bf16[1,192,640]{1,2,0:T(8,128)(2,1)S(1)}, bf16[1,192,640]{1,2,0:T(8,128)(2,1)}, u32[]{:S(2)}) copy-start(bf16[1,192,640]{1,2,0:T(8,128)(2,1)} %copy.26) | copy-start | bytes 737284
  174.4 2.5 copy-start.6
  176.9 52.1 %copy-start.5 = (bf16[192,1,5,128]{3,0,2,1:T(8,128)(2,1)S(1)}, bf16[192,1,5,128]{3,0,2,1:T(8,128)(2,1)}, u32[]{:S(2)}) copy-start(bf16[192,1,5,128]{3,0,2,1:T(8,128)(2,1)} %get-tuple-element.19) | copy-start | bytes 737284
  180.2 565.8 %reduce-scatter.10.cloned.1.call-start = ((), (), s32[]{:S(2)}) async-start(), calls=%async_computation.5 | async-start | bytes 2662400
Sparse Core Ops, SparseCore 0:
  93.0 129.8 reduce-scatter.7
  227.5 107.0 reduce-scatter.5
  338.0 407.9 reduce-scatter.9
where the time goes:
time: 753 us
  waiting for transfers between devices  553 us (73%)
  blocking collectives  128 us (17%)
  matrix products  35 us (5%)
  local copies, waits for them, and re-layouts  17.8 us (2%)
  between operations  13.9 us (2%)
    unnamed x4, waiting for transfers between devices  411 us
    reduce_scatter x1, waiting for transfers between devices, on_device(): lax.psum_scatter(key_part.astype(jnp.bfloat16), 'context', scatter_dimens...  99.1 us
    all_gather x1, blocking collectives, on_device(): lax.all_gather(keys[0], 'context', axis=0, tiled=True)  66.6 us
    all_gather x1, blocking collectives, on_device(): lax.all_gather(values, 'context', axis=0, tiled=True)  61.6 us
    reduce_scatter x1, waiting for transfers between devices, on_device(): lax.psum_scatter(value_part.astype(jnp.bfloat16), 'context', scatter_dime...  42.6 us
  transfers between devices with their start and end apart: 3, of which 3 were waited for; matrix products, arithmetic and copies ran while one was open for 5% of the time, Pallas kernels for 0%

commit v1 on v0

v1 whole, which is shorter than its diff:
```python
import math

import jax
import jax.numpy as jnp
from jax import lax
from jax.experimental import pallas as pl
from jax.experimental.pallas import tpu as pltpu
from jax.sharding import PartitionSpec as P

MESH = pl.DeviceIdType.MESH
BF = jnp.bfloat16
F32 = jnp.float32

HD = 128
TOK = 192
HALF = TOK // 2
HEADS = 5
D = 5120
SEQ = 3072
NX = 4
NZ = 4
NDP = 4
SPAN = 8
LANES = 1024
CHUNK = 256
ROWS_X = D // (NDP * NX)
ROWS_OUT = ROWS_X // NZ
SCALE = HD ** (-0.5)
LOG2E = math.log2(math.e)
NEG = -1e30


def dot(a, b):
    return jnp.dot(a, b, preferred_element_type=F32)


def remote(src, dst, send, recv, device):
    return pltpu.make_async_remote_copy(
        src_ref=src, dst_ref=dst, send_sem=send, recv_sem=recv, device_id=device, device_id_type=MESH
    )


def kernel(
    q_hbm, k_hbm, mem_hbm, w_hbm, doc_hbm, g_hbm,
    att_hbm, gq_hbm, gk_hbm, gw_hbm,
    q_in, g_in, mem, w, doc,
    kv, qall, gall, gnorm, qt, gt, memt,
    sbuf, pbuf, top, total, ot, dqt, out_rows, grad_rows,
    part, from_x, acc, zsend, from_z, gk_out, dv,
    wsend, wown, wrecv, dsend, dacc, drecv, hsend, hrecv, gw_out,
    lsem, gs, gr, xs, xr, zs, zr, ws, wr, ds, dr, hs, hr,
):
    c = lax.axis_index("context")
    dp = lax.axis_index("dp")
    x = c // NZ
    zh = c % NZ

    def zat(j):
        return lax.rem(zh + j, NZ)

    def zdev(j):
        return {"context": x * NZ + zat(j)}

    def xdev(j):
        return {"context": lax.rem(c + NZ * j, NX * NZ)}

    def dpdev(j):
        return {"dp": lax.rem(dp + j, NDP)}

    loads = [
        pltpu.make_async_copy(k_hbm.at[0], kv.at[0, 0, zh], lsem.at[0]),
        pltpu.make_async_copy(mem_hbm.at[0], mem, lsem.at[1]),
        pltpu.make_async_copy(w_hbm, w, lsem.at[2]),
        pltpu.make_async_copy(q_hbm.at[0], q_in, lsem.at[3]),
        pltpu.make_async_copy(g_hbm.at[0], g_in, lsem.at[4]),
        pltpu.make_async_copy(doc_hbm, doc, lsem.at[5]),
    ]
    for load in loads:
        load.start()

    barrier = pltpu.get_barrier_semaphore()
    for j in range(1, 4):
        for device in (zdev(j), xdev(j), dpdev(j)):
            pl.semaphore_signal(barrier, inc=1, device_id=device, device_id_type=MESH)

    def ring(a, i):
        row = kv.at[a, 0]
        if i == 0:
            return remote(row.at[zh], row.at[zh], gs.at[a, 0], gr.at[a, 0], zdev(1))
        if i == 1:
            return remote(row.at[zh], row.at[zh], gs.at[a, 1], gr.at[a, 1], zdev(3))
        if i == 2:
            half = row.at[zat(3), pl.ds(0, HALF)]
            return remote(half, half, gs.at[a, 2], gr.at[a, 2], zdev(1))
        half = row.at[zat(1), pl.ds(HALF, HALF)]
        return remote(half, half, gs.at[a, 3], gr.at[a, 3], zdev(3))

    def down(a, r, j):
        z = zat(j)
        return remote(
            kv.at[a, 0, z], kv.at[a, r, z], gs.at[a, 4 * r + j], gr.at[a, 4 * r + j], xdev(r)
        )

    def down_all(a, j, act):
        @pl.when(x < NX - 1)
        def _():
            act(down(a, 1, j))

        @pl.when((x < NX - 2) & (zat(j) >= zh))
        def _():
            act(down(a, 2, j))

    def from_above(a):
        for j in range(NZ):
            @pl.when(x > 0)
            def _():
                down(a, 1, j).wait_recv()

            @pl.when((x > 1) & (zat(j) >= zh))
            def _():
                down(a, 2, j).wait_recv()

    def start(copy):
        copy.start()

    def wait_send(copy):
        copy.wait_send()

    loads[0].wait()
    pl.semaphore_wait(barrier, 9)
    ring(0, 0).start()
    ring(0, 1).start()
    down_all(0, 0, start)

    loads[1].wait()
    loads[2].wait()
    kv[1, 0, zh] = dot(mem[...], w[...]).astype(BF)
    ring(1, 0).start()
    ring(1, 1).start()
    down_all(1, 0, start)

    loads[3].wait()
    loads[4].wait()
    loads[5].wait()
    for h in range(HEADS):
        qall[TOK * h : TOK * (h + 1), :] = q_in[:, HD * h : HD * (h + 1)]
        gall[TOK * h : TOK * (h + 1), :] = g_in[:, HD * h : HD * (h + 1)]
    pad = jnp.zeros((LANES - HEADS * TOK, HD), BF)
    qall[HEADS * TOK :, :] = pad
    gall[HEADS * TOK :, :] = pad
    qt[...] = qall[...].T
    gt[...] = gall[...].T

    doc_row = doc[...].astype(F32)
    pair = doc[:, pl.ds(pl.multiple_of(2 * TOK * (c // 2), 128), 2 * TOK)].astype(F32)
    doc_q = jnp.where(c % 2 == 0, pair[:, :TOK], pair[:, TOK:])
    first = jnp.zeros((1, TOK), F32)
    for d in range(1, 8):
        before = jnp.sum(jnp.where(doc_row < d, 1.0, 0.0), axis=1, keepdims=True)
        first = jnp.where(doc_q == d, before, first)
    own_pos = lax.broadcasted_iota(jnp.int32, (1, TOK), 1).astype(F32) + (c * TOK).astype(F32)
    lane_pad = LANES - HEADS * TOK
    q_first = jnp.concatenate([first] * HEADS + [jnp.zeros((1, lane_pad), F32)], axis=1)
    q_pos = jnp.concatenate([own_pos] * HEADS + [jnp.full((1, lane_pad), float(SEQ), F32)], axis=1)

    part[:, 0] = jnp.zeros((2, NZ, TOK, HD), BF)
    top[...] = jnp.full((8, LANES), NEG, F32)
    total[...] = jnp.zeros((8, LANES), F32)

    blocks = jnp.minimum(c, SPAN) + 1

    def slot(d):
        b = c - d
        return x - b // NZ, b % NZ

    def scores(d, carry):
        r, z = slot(d)
        kb = kv[0, r, z]
        key_pos = lax.broadcasted_iota(jnp.int32, (TOK, CHUNK), 0).astype(F32) + (
            (c - d) * TOK
        ).astype(F32)
        for i in range(LANES // CHUNK):
            at = slice(CHUNK * i, CHUNK * (i + 1))
            s = dot(kb, qt[:, at])
            s = jnp.where((key_pos >= q_first[:, at]) & (key_pos <= q_pos[:, at]), s, NEG)
            sbuf[d, :, at] = s
            top[:, at] = jnp.maximum(top[:, at], jnp.max(s.reshape(TOK // 8, 8, CHUNK), axis=0))
        return carry

    ring(0, 0).wait_recv()
    ring(0, 2).start()
    ring(0, 1).wait_recv()
    ring(0, 3).start()
    down_all(0, 1, start)
    down_all(0, 3, start)
    ring(1, 0).wait_recv()
    ring(1, 2).start()
    ring(1, 1).wait_recv()
    ring(1, 3).start()
    down_all(1, 1, start)
    down_all(1, 3, start)
    ring(0, 2).wait_recv()
    ring(0, 3).wait_recv()
    down_all(0, 2, start)
    lax.fori_loop(0, jnp.minimum(zh + 1, blocks), scores, 0)
    memt[...] = mem[...].T
    ring(1, 2).wait_recv()
    ring(1, 3).wait_recv()
    down_all(1, 2, start)
    from_above(0)
    lax.fori_loop(jnp.minimum(zh + 1, blocks), blocks, scores, 0)

    top_row = jnp.max(top[...], axis=0, keepdims=True) * (SCALE * LOG2E)

    def numerators(d, carry):
        for i in range(LANES // CHUNK):
            at = slice(CHUNK * i, CHUNK * (i + 1))
            e = jnp.exp2(sbuf[d, :, at] * (SCALE * LOG2E) - top_row[:, at])
            sbuf[d, :, at] = e
            pbuf[d, :, at] = e.astype(BF)
            total[:, at] += jnp.sum(e.reshape(TOK // 8, 8, CHUNK), axis=0)
        return carry

    lax.fori_loop(0, blocks, numerators, 0)
    inv = 1.0 / jnp.sum(total[...], axis=0, keepdims=True)
    inv_col = jnp.broadcast_to(inv, (HD, LANES)).T
    gnorm[...] = (gall[...].astype(F32) * inv_col).astype(BF)

    def up(a, r, j):
        z = zat(j)
        return remote(
            part.at[a, r, z], from_x.at[a, r - 1, z], xs.at[a, 4 * (r - 1) + j],
            xr.at[a, 4 * (r - 1) + j], xdev(NX - r),
        )

    def up_all(a, act):
        for j in range(NZ):
            @pl.when(x > 0)
            def _():
                act(up(a, 1, j))

            @pl.when((x > 1) & (zat(j) >= zh))
            def _():
                act(up(a, 2, j))

    def over(a, j):
        return remote(zsend.at[a, zat(j)], from_z.at[a, j], zs.at[a, j], zr.at[a, j], zdev(j))

    def sum_rows(a):
        for j in (2, 1, 3, 0):
            z = zat(j)
            acc[...] = part[a, 0, z].astype(F32)

            @pl.when(x < NX - 1)
            def _():
                up(a, 1, j).wait_recv()
                acc[...] += from_x[a, 0, z].astype(F32)

            @pl.when((x < NX - 2) & (z >= zh))
            def _():
                up(a, 2, j).wait_recv()
                acc[...] += from_x[a, 1, z].astype(F32)

            if j:
                zsend[a, z] = acc[...].astype(BF)
                over(a, j).start()
            else:
                part[a, 0, z] = acc[...].astype(BF)

    def sum_ring(a):
        out = part[a, 0, zh].astype(F32)
        for j in (1, 3, 2):
            over(a, j).wait_recv()
            out = out + from_z[a, j].astype(F32)
        return out.astype(BF)

    def value_parts(d, carry):
        r, z = slot(d)
        part[1, r, z] = dot(pbuf[d], gnorm[...]).astype(BF)
        return carry

    lax.fori_loop(0, blocks, value_parts, 0)
    up_all(1, start)

    from_above(1)
    ot[...] = jnp.zeros((HD, LANES), F32)

    def attend(d, carry):
        r, z = slot(d)
        ot[...] += dot(kv[1, r, z].T, pbuf[d])
        return carry

    lax.fori_loop(0, blocks, attend, 0)
    att = (ot[...] * inv).astype(BF).astype(F32)
    delta = jnp.sum(att * gt[...].astype(F32), axis=0, keepdims=True)
    att_rows = att.T.astype(BF)
    for h in range(HEADS):
        out_rows[:, HD * h : HD * (h + 1)] = att_rows[TOK * h : TOK * (h + 1), :]
    store_att = pltpu.make_async_copy(out_rows, att_hbm.at[0], lsem.at[6])
    store_att.start()

    sum_rows(1)

    dqt[...] = jnp.zeros((HD, LANES), F32)
    inv_scaled = inv * SCALE

    def grads(d, carry):
        r, z = slot(d)
        vb = kv[1, r, z]
        kt = kv[0, r, z].T
        for i in range(LANES // CHUNK):
            at = slice(CHUNK * i, CHUNK * (i + 1))
            dprob = dot(vb, gt[:, at])
            pbuf[d, :, at] = (sbuf[d, :, at] * ((dprob - delta[:, at]) * inv_scaled[:, at])).astype(BF)
        part[0, r, z] = dot(pbuf[d], qall[...]).astype(BF)
        dqt[...] += dot(kt, pbuf[d])
        return carry

    lax.fori_loop(0, blocks, grads, 0)
    up_all(0, start)
    dq_rows = dqt[...].T.astype(BF)
    for h in range(HEADS):
        grad_rows[:, HD * h : HD * (h + 1)] = dq_rows[TOK * h : TOK * (h + 1), :]
    store_gq = pltpu.make_async_copy(grad_rows, gq_hbm.at[0], lsem.at[7])
    store_gq.start()

    sum_rows(0)
    dv[...] = sum_ring(1)

    def wx(k, o):
        return remote(wsend.at[k, o], wrecv.at[k, o], ws.at[k, o], wr.at[k, o], xdev(o))

    def wd(k):
        return remote(dsend.at[k], drecv.at[k], ds.at[k], dr.at[k], dpdev(k + 1))

    def wh(o):
        return remote(hsend.at[o], hrecv.at[o], hs.at[o], hr.at[o], zdev(o))

    for k in range(NDP):
        for o in (2, 1, 3, 0):
            row = NX * ROWS_X * lax.rem(dp + 1 + k, NDP) + ROWS_X * lax.rem(x + o, NX)
            piece = dot(memt[pl.ds(pl.multiple_of(row, 64), ROWS_X), :], dv[...])
            if o:
                wsend[k, o] = piece.astype(BF)
                wx(k, o).start()
            else:
                wown[k] = piece

    gk_out[...] = sum_ring(0)
    store_gk = pltpu.make_async_copy(gk_out, gk_hbm.at[0], lsem.at[8])
    store_gk.start()

    for k in range(NDP):
        piece = wown[k]
        for o in (1, 3, 2):
            wx(k, o).wait_recv()
            piece = piece + wrecv[k, o].astype(F32)
        if k < NDP - 1:
            dsend[k] = piece.astype(BF)
            wd(k).start()
        else:
            dacc[...] = piece
    for k in range(NDP - 1):
        wd(k).wait_recv()
        dacc[...] += drecv[k].astype(F32)
    for o in (2, 1, 3):
        rows = pl.ds(pl.multiple_of(ROWS_OUT * zat(o), 16), ROWS_OUT)
        hsend[o] = dacc[rows, :].astype(BF)
        wh(o).start()
    out = dacc[pl.ds(pl.multiple_of(ROWS_OUT * zh, 16), ROWS_OUT), :]
    for o in (1, 3, 2):
        wh(o).wait_recv()
        out = out + hrecv[o].astype(F32)
    gw_out[...] = out
    store_gw = pltpu.make_async_copy(gw_out, gw_hbm, lsem.at[9])
    store_gw.start()

    for a in range(2):
        for i in range(4):
            ring(a, i).wait_send()
        for j in range(NZ):
            down_all(a, j, wait_send)
        up_all(a, wait_send)
        for j in range(1, NZ):
            over(a, j).wait_send()
    for k in range(NDP):
        for o in range(1, NX):
            wx(k, o).wait_send()
    for k in range(NDP - 1):
        wd(k).wait_send()
    for o in range(1, NZ):
        wh(o).wait_send()
    for store in (store_att, store_gq, store_gk, store_gw):
        store.wait()


def on_device(queries, keys, memory, value_weight, doc_ids, out_grad):
    vmem = pltpu.VMEM
    dma = pltpu.SemaphoreType.DMA
    anywhere = pl.BlockSpec(memory_space=pl.ANY)
    shape = jax.ShapeDtypeStruct
    return pl.pallas_call(
        kernel,
        out_shape=(
            shape((1, TOK, HEADS * HD), BF),
            shape((1, TOK, HEADS * HD), BF),
            shape((1, TOK, HD), BF),
            shape((ROWS_OUT, HD), F32),
        ),
        in_specs=[anywhere] * 6,
        out_specs=(anywhere,) * 4,
        scratch_shapes=[
            vmem((TOK, HEADS * HD), BF),
            vmem((TOK, HEADS * HD), BF),
            vmem((TOK, D), BF),
            vmem((D, HD), BF),
            vmem((1, SEQ), jnp.int32),
            vmem((2, 3, NZ, TOK, HD), BF),
            vmem((LANES, HD), BF),
            vmem((LANES, HD), BF),
            vmem((LANES, HD), BF),
            vmem((HD, LANES), BF),
            vmem((HD, LANES), BF),
            vmem((D, TOK), BF),
            vmem((SPAN + 1, TOK, LANES), F32),
            vmem((SPAN + 1, TOK, LANES), BF),
            vmem((8, LANES), F32),
            vmem((8, LANES), F32),
            vmem((HD, LANES), F32),
            vmem((HD, LANES), F32),
            vmem((TOK, HEADS * HD), BF),
            vmem((TOK, HEADS * HD), BF),
            vmem((2, 3, NZ, TOK, HD), BF),
            vmem((2, 2, NZ, TOK, HD), BF),
            vmem((TOK, HD), F32),
            vmem((2, NZ, TOK, HD), BF),
            vmem((2, NZ, TOK, HD), BF),
            vmem((TOK, HD), BF),
            vmem((TOK, HD), BF),
            vmem((NDP, NX, ROWS_X, HD), BF),
            vmem((NDP, ROWS_X, HD), F32),
            vmem((NDP, NX, ROWS_X, HD), BF),
            vmem((NDP, ROWS_X, HD), BF),
            vmem((ROWS_X, HD), F32),
            vmem((NDP, ROWS_X, HD), BF),
            vmem((NZ, ROWS_OUT, HD), BF),
            vmem((NZ, ROWS_OUT, HD), BF),
            vmem((ROWS_OUT, HD), F32),
            dma((10,)),
            dma((2, 12)), dma((2, 12)),
            dma((2, 8)), dma((2, 8)),
            dma((2, NZ)), dma((2, NZ)),
            dma((NDP, NX)), dma((NDP, NX)),
            dma((NDP,)), dma((NDP,)),
            dma((NZ,)), dma((NZ,)),
        ],
        compiler_params=pltpu.CompilerParams(
            collective_id=0, has_side_effects=True, vmem_limit_bytes=48 << 20
        ),
        name="cross_attention",
    )(queries, keys, memory, value_weight, doc_ids, out_grad)


def solution(mesh):
    in_specs = (
        P("dp", "context", "tensor"),
        P("dp", "context", "tensor"),
        P("dp", "context", None),
        P(None, "tensor"),
        P("dp", None),
        P("dp", "context", "tensor"),
    )
    out_specs = (
        P("dp", "context", "tensor"),
        P("dp", "context", "tensor"),
        P("dp", "context", "tensor"),
        P(("dp", "context"), "tensor"),
    )
    return jax.shard_map(
        on_device, mesh=mesh, in_specs=in_specs, out_specs=out_specs, check_vma=False
    )
```

time: 753 us -> 96.8 us (0.13)
  the two profiles are of different devices: /device:TPU:56 before, /device:TPU:26 now
where the time goes in v1:
time: 96.8 us; the launch traced here: 96.5 us
  Pallas kernels  86.9 us (90%)
  local copies, waits for them, and re-layouts  8.87 us (9%)
    pallas_call x1, Pallas kernels, on_device(): pl.pallas_call(kernel, out_shape=(shape((1, TOK, HEADS * HD), BF), shape(...  86.9 us
    unnamed x16, local copies, waits for them, and re-layouts  8.87 us

profile of v1, /device:TPU:26, one launch (start us, length us, event | category | flops | bytes accessed | tf_op | source)
XLA Modules:
  0.0 96.5 jit_solution(7749211334930748457)
XLA Ops:
  0.6 0.0 copy-start
  0.6 1.5 %copy-done = bf16[1,192,5120]{2,1,0:T(8,128)(2,1)S(1)} copy-done((bf16[1,192,5120]{2,1,0:T(8,128)(2,1)S(1)}, bf16[1,192,5120]{2,1,0:T(8,128)(2,1)}, u32[]{:S(2)}) %copy-start) | copy-done | bytes 1966104
  2.2 0.0 copy-start.1
  2.2 1.3 %copy-done.1 = bf16[5120,128]{1,0:T(8,128)(2,1)S(1)} copy-done((bf16[5120,128]{1,0:T(8,128)(2,1)S(1)}, bf16[5120,128]{1,0:T(8,128)(2,1)}, u32[]{:S(2)}) %copy-start.1) | copy-done | bytes 1310744
  3.5 0.0 copy-start.2
  3.5 0.9 copy-done.2
  4.4 0.0 copy-start.3
  4.4 0.9 copy-done.3
  5.4 0.0 copy-start.4
  5.4 0.8 copy-done.4
  6.2 0.0 copy-start.5
  6.2 0.7 copy-done.5
  6.9 86.9 %cross_attention.1 = (bf16[1,192,640]{2,1,0:T(8,128)(2,1)S(1)}, bf16[1,192,640]{2,1,0:T(8,128)(2,1)S(1)}, bf16[1,192,128]{2,1,0:T(8,128)(2,1)S(1)}, f32[80,128]{1,0:T(8,128)S(1)}) custom-call(bf16[1,192,640]{2,1,0:T(8,128)(2,1)S(1)} %copy-done.2, bf16[1,192,128]{2,1,0:T(8,128)(2,1)S(1)} %copy-done.4, bf16[1,192,5120]{2,1,0:T(8,128)(2,1)S(1)} %copy-done, ...), custom_call_target="tpu_custom_call" | custom-call | tf_op jit(solution)/shard_map/cross_attention/pallas_call | solution.py:402
  93.8 0.7 copy.14
  94.5 0.7 copy.15
  95.2 0.6 copy.16
  95.8 0.6 copy.17
Async XLA Ops:
  0.6 1.5 %copy-start = (bf16[1,192,5120]{2,1,0:T(8,128)(2,1)S(1)}, bf16[1,192,5120]{2,1,0:T(8,128)(2,1)}, u32[]{:S(2)}) copy-start(bf16[1,192,5120]{2,1,0:T(8,128)(2,1)} %mem_hbm.1) | copy-start | bytes 5898244
  2.2 1.3 %copy-start.1 = (bf16[5120,128]{1,0:T(8,128)(2,1)S(1)}, bf16[5120,128]{1,0:T(8,128)(2,1)}, u32[]{:S(2)}) copy-start(bf16[5120,128]{1,0:T(8,128)(2,1)} %w_hbm.1) | copy-start | bytes 3932164
  3.5 0.9 copy-start.2
  4.4 0.9 copy-start.3
  5.4 0.8 copy-start.4
  6.2 0.7 copy-start.5

commit v2 on v1

--- a/solution.py
+++ b/solution.py
@@ -173,8 +173,13 @@
         b = c - d
         return x - b // NZ, b % NZ
 
-    def scores(d, carry):
-        r, z = slot(d)
+    def there(r, j):
+        z = zat(j)
+        return (z <= zh, x > 0, (x > 1) & (z >= zh))[r]
+
+    def scores(r, j):
+        z = zat(j)
+        d = NZ * r + zh - z
         kb = kv[0, r, z]
         key_pos = lax.broadcasted_iota(jnp.int32, (TOK, CHUNK), 0).astype(F32) + (
             (c - d) * TOK
@@ -185,7 +190,29 @@
             s = jnp.where((key_pos >= q_first[:, at]) & (key_pos <= q_pos[:, at]), s, NEG)
             sbuf[d, :, at] = s
             top[:, at] = jnp.maximum(top[:, at], jnp.max(s.reshape(TOK // 8, 8, CHUNK), axis=0))
+
+    def by_arrival(i):
+        return jnp.where(i == 2, 3, jnp.where(i == 3, 2, i))
+
+    def own_scores(j, carry):
+        @pl.when(there(0, j))
+        def _():
+            scores(0, j)
+
         return carry
+
+    def far_scores(r):
+        def step(i, carry):
+            j = by_arrival(i)
+
+            @pl.when(there(r, j))
+            def _():
+                down(0, r, j).wait_recv()
+                scores(r, j)
+
+            return carry
+
+        return step
 
     ring(0, 0).wait_recv()
     ring(0, 2).start()
@@ -202,13 +229,12 @@
     ring(0, 2).wait_recv()
     ring(0, 3).wait_recv()
     down_all(0, 2, start)
-    lax.fori_loop(0, jnp.minimum(zh + 1, blocks), scores, 0)
-    memt[...] = mem[...].T
+    lax.fori_loop(0, NZ, own_scores, 0)
     ring(1, 2).wait_recv()
     ring(1, 3).wait_recv()
     down_all(1, 2, start)
-    from_above(0)
-    lax.fori_loop(jnp.minimum(zh + 1, blocks), blocks, scores, 0)
+    lax.fori_loop(0, NZ, far_scores(1), 0)
+    lax.fori_loop(0, NZ, far_scores(2), 0)
 
     top_row = jnp.max(top[...], axis=0, keepdims=True) * (SCALE * LOG2E)
 
@@ -274,13 +300,22 @@
             out = out + from_z[a, j].astype(F32)
         return out.astype(BF)
 
-    def value_parts(d, carry):
-        r, z = slot(d)
-        part[1, r, z] = dot(pbuf[d], gnorm[...]).astype(BF)
-        return carry
-
-    lax.fori_loop(0, blocks, value_parts, 0)
-    up_all(1, start)
+    def value_parts(r):
+        def step(j, carry):
+            z = zat(j)
+
+            @pl.when(there(r, j))
+            def _():
+                part[1, r, z] = dot(pbuf[NZ * r + zh - z], gnorm[...]).astype(BF)
+                if r:
+                    up(1, r, j).start()
+
+            return carry
+
+        return step
+
+    for r in (2, 1, 0):
+        lax.fori_loop(0, NZ, value_parts(r), 0)
 
     from_above(1)
     ot[...] = jnp.zeros((HD, LANES), F32)
@@ -304,8 +339,9 @@
     dqt[...] = jnp.zeros((HD, LANES), F32)
     inv_scaled = inv * SCALE
 
-    def grads(d, carry):
-        r, z = slot(d)
+    def grads(r, j):
+        z = zat(j)
+        d = NZ * r + zh - z
         vb = kv[1, r, z]
         kt = kv[0, r, z].T
         for i in range(LANES // CHUNK):
@@ -314,17 +350,28 @@
             pbuf[d, :, at] = (sbuf[d, :, at] * ((dprob - delta[:, at]) * inv_scaled[:, at])).astype(BF)
         part[0, r, z] = dot(pbuf[d], qall[...]).astype(BF)
         dqt[...] += dot(kt, pbuf[d])
-        return carry
-
-    lax.fori_loop(0, blocks, grads, 0)
-    up_all(0, start)
+
+    def grad_parts(r):
+        def step(j, carry):
+            @pl.when(there(r, j))
+            def _():
+                grads(r, j)
+                if r:
+                    up(0, r, j).start()
+
+            return carry
+
+        return step
+
+    for r in (2, 1, 0):
+        lax.fori_loop(0, NZ, grad_parts(r), 0)
     dq_rows = dqt[...].T.astype(BF)
     for h in range(HEADS):
         grad_rows[:, HD * h : HD * (h + 1)] = dq_rows[TOK * h : TOK * (h + 1), :]
     store_gq = pltpu.make_async_copy(grad_rows, gq_hbm.at[0], lsem.at[7])
     store_gq.start()
 
-    sum_rows(0)
+    memt[...] = mem[...].T
     dv[...] = sum_ring(1)
 
     def wx(k, o):
@@ -346,9 +393,7 @@
             else:
                 wown[k] = piece
 
-    gk_out[...] = sum_ring(0)
-    store_gk = pltpu.make_async_copy(gk_out, gk_hbm.at[0], lsem.at[8])
-    store_gk.start()
+    sum_rows(0)
 
     for k in range(NDP):
         piece = wown[k]
@@ -367,6 +412,10 @@
         rows = pl.ds(pl.multiple_of(ROWS_OUT * zat(o), 16), ROWS_OUT)
         hsend[o] = dacc[rows, :].astype(BF)
         wh(o).start()
+    gk_out[...] = sum_ring(0)
+    store_gk = pltpu.make_async_copy(gk_out, gk_hbm.at[0], lsem.at[8])
+    store_gk.start()
+
     out = dacc[pl.ds(pl.multiple_of(ROWS_OUT * zh, 16), ROWS_OUT), :]
     for o in (1, 3, 2):
         wh(o).wait_recv()
@@ -394,12 +443,24 @@
         store.wait()
 
 
+def hand_over(*refs):
+    into = [pltpu.make_async_copy(refs[i], refs[8 + i], refs[12].at[i]) for i in range(4)]
+    back = [pltpu.make_async_copy(refs[8 + i], refs[4 + i], refs[13].at[i]) for i in range(4)]
+    for copy in into:
+        copy.start()
+    for i in range(4):
+        into[i].wait()
+        back[i].start()
+    for copy in back:
+        copy.wait()
+
+
 def on_device(queries, keys, memory, value_weight, doc_ids, out_grad):
     vmem = pltpu.VMEM
     dma = pltpu.SemaphoreType.DMA
     anywhere = pl.BlockSpec(memory_space=pl.ANY)
     shape = jax.ShapeDtypeStruct
-    return pl.pallas_call(
+    outs = pl.pallas_call(
         kernel,
         out_shape=(
             shape((1, TOK, HEADS * HD), BF),
@@ -407,7 +468,7 @@
             shape((1, TOK, HD), BF),
             shape((ROWS_OUT, HD), F32),
         ),
-        in_specs=[anywhere] * 6,
+        in_specs=[pl.BlockSpec(memory_space=pltpu.HBM)] * 6,
         out_specs=(anywhere,) * 4,
         scratch_shapes=[
             vmem((TOK, HEADS * HD), BF),
@@ -455,10 +516,19 @@
             dma((NZ,)), dma((NZ,)),
         ],
         compiler_params=pltpu.CompilerParams(
-            collective_id=0, has_side_effects=True, vmem_limit_bytes=48 << 20
+            collective_id=0, has_side_effects=True, vmem_limit_bytes=60 << 20
         ),
         name="cross_attention",
     )(queries, keys, memory, value_weight, doc_ids, out_grad)
+    return pl.pallas_call(
+        hand_over,
+        out_shape=tuple(shape(o.shape, o.dtype) for o in outs),
+        in_specs=[anywhere] * 4,
+        out_specs=(anywhere,) * 4,
+        scratch_shapes=[*(vmem(o.shape, o.dtype) for o in outs), dma((4,)), dma((4,))],
+        compiler_params=pltpu.CompilerParams(vmem_limit_bytes=60 << 20),
+        name="hand_over",
+    )(*outs)
 
 
 def solution(mesh):

time: 96.8 us -> 82 us (0.85)
  local copies, waits for them, and re-layouts: 8.87 us -> 0 us
  Pallas kernels: 86.9 us -> 81.2 us
    unnamed x16 -> x0, local copies, waits for them, and re-layouts: 8.87 us -> none
    pallas_call x1, Pallas kernels: 86.9 us -> 79.4 us  [on_device(): pl.pallas_call(kernel, out_shape=(shape((1, TOK, HEADS * HD), BF), shape(...]
    pallas_call x0 -> x1, Pallas kernels: none -> 1.85 us  [on_device(): pl.pallas_call(hand_over, out_shape=tuple((shape(o.shape, o.dtype) for o...]
where the time goes in v2:
time: 82 us; the launch traced here: 81.9 us
  Pallas kernels  81.2 us (99%)
    pallas_call x1, Pallas kernels, on_device(): pl.pallas_call(kernel, out_shape=(shape((1, TOK, HEADS * HD), BF), shape(...  79.4 us
    pallas_call x1, Pallas kernels, on_device(): pl.pallas_call(hand_over, out_shape=tuple((shape(o.shape, o.dtype) for o...  1.85 us

profile of v2, /device:TPU:26, one launch (start us, length us, event | category | flops | bytes accessed | tf_op | source)
XLA Modules:
  0.0 81.9 jit_solution(13956484820484261415)
XLA Ops:
  0.6 79.4 %cross_attention.1 = (bf16[1,192,640]{2,1,0:T(8,128)(2,1)}, bf16[1,192,640]{2,1,0:T(8,128)(2,1)}, bf16[1,192,128]{2,1,0:T(8,128)(2,1)}, f32[80,128]{1,0:T(8,128)}) custom-call(bf16[1,192,640]{2,1,0:T(8,128)(2,1)} %q_hbm.1, bf16[1,192,128]{2,1,0:T(8,128)(2,1)} %k_hbm.1, bf16[1,192,5120]{2,1,0:T(8,128)(2,1)} %mem_hbm.1, bf16[5120,128]{1,0:T(8,128)(2,1)} %w_hbm.1, ...), custom_call_target="tpu_custom_call" | custom-call | tf_op jit(solution)/shard_map/cross_attention/pallas_call | solution.py:463
  80.0 1.8 %hand_over.1 = (bf16[1,192,640]{2,1,0:T(8,128)(2,1)}, bf16[1,192,640]{2,1,0:T(8,128)(2,1)}, bf16[1,192,128]{2,1,0:T(8,128)(2,1)}, f32[80,128]{1,0:T(8,128)}) custom-call(bf16[1,192,640]{2,1,0:T(8,128)(2,1)} %get-tuple-element.8.refs_0_, bf16[1,192,640]{2,1,0:T(8,128)(2,1)} %get-tuple-element.9.refs_1_, bf16[1,192,128]{2,1,0:T(8,128)(2,1)} %get-tuple-element.10.refs_2_, ...), custom_call_target="tpu_custom_call" | custom-call | tf_op jit(solution)/shard_map/hand_over/pallas_call | solution.py:523

commit v3 on v2

--- a/solution.py
+++ b/solution.py
@@ -21,6 +21,9 @@
 NZ = 4
 NDP = 4
 SPAN = 8
+BLOCKS = SPAN + 1
+SLOTS = BLOCKS + NZ - 1
+GROUP = 3
 LANES = 1024
 CHUNK = 256
 ROWS_X = D // (NDP * NX)
@@ -34,6 +37,10 @@
     return jnp.dot(a, b, preferred_element_type=F32)
 
 
+def dot_rows(a, b):
+    return lax.dot_general(a, b, (((0,), (0,)), ((), ())), preferred_element_type=F32)
+
+
 def remote(src, dst, send, recv, device):
     return pltpu.make_async_remote_copy(
         src_ref=src, dst_ref=dst, send_sem=send, recv_sem=recv, device_id=device, device_id_type=MESH
@@ -46,9 +53,9 @@
     q_in, g_in, mem, w, doc,
     kv, qall, gall, gnorm, qt, gt, memt,
     sbuf, pbuf, top, total, ot, dqt, out_rows, grad_rows,
-    part, from_x, acc, zsend, from_z, gk_out, dv,
+    part, from_x, acc, zown, zsend, from_z, gk_out, dv,
     wsend, wown, wrecv, dsend, dacc, drecv, hsend, hrecv, gw_out,
-    lsem, gs, gr, xs, xr, zs, zr, ws, wr, ds, dr, hs, hr,
+    lsem, cs, cr, gs, gr, xs, xr, zs, zr, ws, wr, ds, dr, hs, hr,
 ):
     c = lax.axis_index("context")
     dp = lax.axis_index("dp")
@@ -68,7 +75,7 @@
         return {"dp": lax.rem(dp + j, NDP)}
 
     loads = [
-        pltpu.make_async_copy(k_hbm.at[0], kv.at[0, 0, zh], lsem.at[0]),
+        pltpu.make_async_copy(k_hbm.at[0], kv.at[0, 0], lsem.at[0]),
         pltpu.make_async_copy(mem_hbm.at[0], mem, lsem.at[1]),
         pltpu.make_async_copy(w_hbm, w, lsem.at[2]),
         pltpu.make_async_copy(q_hbm.at[0], q_in, lsem.at[3]),
@@ -83,23 +90,23 @@
         for device in (zdev(j), xdev(j), dpdev(j)):
             pl.semaphore_signal(barrier, inc=1, device_id=device, device_id_type=MESH)
 
+    def slot(z, h):
+        e = h - z
+        return jnp.where(e < 0, e + SLOTS, e)
+
     def ring(a, i):
-        row = kv.at[a, 0]
-        if i == 0:
-            return remote(row.at[zh], row.at[zh], gs.at[a, 0], gr.at[a, 0], zdev(1))
-        if i == 1:
-            return remote(row.at[zh], row.at[zh], gs.at[a, 1], gr.at[a, 1], zdev(3))
-        if i == 2:
-            half = row.at[zat(3), pl.ds(0, HALF)]
-            return remote(half, half, gs.at[a, 2], gr.at[a, 2], zdev(1))
-        half = row.at[zat(1), pl.ds(HALF, HALF)]
-        return remote(half, half, gs.at[a, 3], gr.at[a, 3], zdev(3))
+        to = (1, 3)[i % 2]
+        z = (zh, zh, zat(3), zat(1))[i]
+        rows = (pl.ds(0, TOK), pl.ds(0, TOK), pl.ds(0, HALF), pl.ds(HALF, HALF))[i]
+        return remote(
+            kv.at[a, slot(z, zh), rows], kv.at[a, slot(z, zat(to)), rows],
+            cs.at[a, i], cr.at[a, i], zdev(to),
+        )
 
     def down(a, r, j):
         z = zat(j)
-        return remote(
-            kv.at[a, 0, z], kv.at[a, r, z], gs.at[a, 4 * r + j], gr.at[a, 4 * r + j], xdev(r)
-        )
+        d = NZ * r + zh - z
+        return remote(kv.at[a, slot(z, zh)], kv.at[a, d], gs.at[a, d], gr.at[a, d], xdev(r))
 
     def down_all(a, j, act):
         @pl.when(x < NX - 1)
@@ -110,15 +117,11 @@
         def _():
             act(down(a, 2, j))
 
-    def from_above(a):
-        for j in range(NZ):
-            @pl.when(x > 0)
+    def from_above(a, d):
+        if d:
+            @pl.when((d > zh) & (d <= c))
             def _():
-                down(a, 1, j).wait_recv()
-
-            @pl.when((x > 1) & (zat(j) >= zh))
-            def _():
-                down(a, 2, j).wait_recv()
+                remote(kv.at[a, d], kv.at[a, d], gs.at[a, d], gr.at[a, d], xdev(1)).wait_recv()
 
     def start(copy):
         copy.start()
@@ -134,7 +137,7 @@
 
     loads[1].wait()
     loads[2].wait()
-    kv[1, 0, zh] = dot(mem[...], w[...]).astype(BF)
+    kv[1, 0] = dot(mem[...], w[...]).astype(BF)
     ring(1, 0).start()
     ring(1, 1).start()
     down_all(1, 0, start)
@@ -163,56 +166,26 @@
     q_first = jnp.concatenate([first] * HEADS + [jnp.zeros((1, lane_pad), F32)], axis=1)
     q_pos = jnp.concatenate([own_pos] * HEADS + [jnp.full((1, lane_pad), float(SEQ), F32)], axis=1)
 
-    part[:, 0] = jnp.zeros((2, NZ, TOK, HD), BF)
     top[...] = jnp.full((8, LANES), NEG, F32)
     total[...] = jnp.zeros((8, LANES), F32)
 
-    blocks = jnp.minimum(c, SPAN) + 1
-
-    def slot(d):
-        b = c - d
-        return x - b // NZ, b % NZ
-
-    def there(r, j):
-        z = zat(j)
-        return (z <= zh, x > 0, (x > 1) & (z >= zh))[r]
-
-    def scores(r, j):
-        z = zat(j)
-        d = NZ * r + zh - z
-        kb = kv[0, r, z]
+    for d in range(1, BLOCKS):
+        @pl.when(d > c)
+        def _():
+            kv[:, d] = jnp.zeros((2, TOK, HD), BF)
+
+    def scores(d):
+        kb = kv[0, d]
         key_pos = lax.broadcasted_iota(jnp.int32, (TOK, CHUNK), 0).astype(F32) + (
             (c - d) * TOK
         ).astype(F32)
+        rows = slice(TOK * d, TOK * (d + 1))
         for i in range(LANES // CHUNK):
             at = slice(CHUNK * i, CHUNK * (i + 1))
             s = dot(kb, qt[:, at])
             s = jnp.where((key_pos >= q_first[:, at]) & (key_pos <= q_pos[:, at]), s, NEG)
-            sbuf[d, :, at] = s
+            sbuf[rows, at] = s
             top[:, at] = jnp.maximum(top[:, at], jnp.max(s.reshape(TOK // 8, 8, CHUNK), axis=0))
-
-    def by_arrival(i):
-        return jnp.where(i == 2, 3, jnp.where(i == 3, 2, i))
-
-    def own_scores(j, carry):
-        @pl.when(there(0, j))
-        def _():
-            scores(0, j)
-
-        return carry
-
-    def far_scores(r):
-        def step(i, carry):
-            j = by_arrival(i)
-
-            @pl.when(there(r, j))
-            def _():
-                down(0, r, j).wait_recv()
-                scores(r, j)
-
-            return carry
-
-        return step
 
     ring(0, 0).wait_recv()
     ring(0, 2).start()
@@ -229,45 +202,47 @@
     ring(0, 2).wait_recv()
     ring(0, 3).wait_recv()
     down_all(0, 2, start)
-    lax.fori_loop(0, NZ, own_scores, 0)
+    scores(0)
     ring(1, 2).wait_recv()
     ring(1, 3).wait_recv()
     down_all(1, 2, start)
-    lax.fori_loop(0, NZ, far_scores(1), 0)
-    lax.fori_loop(0, NZ, far_scores(2), 0)
+    for d in (4, 8, 1, 3, 5, 7, 2, 6):
+        from_above(0, d)
+        scores(d)
 
     top_row = jnp.max(top[...], axis=0, keepdims=True) * (SCALE * LOG2E)
 
     def numerators(d, carry):
+        rows = pl.ds(pl.multiple_of(TOK * d, TOK), TOK)
         for i in range(LANES // CHUNK):
             at = slice(CHUNK * i, CHUNK * (i + 1))
-            e = jnp.exp2(sbuf[d, :, at] * (SCALE * LOG2E) - top_row[:, at])
-            sbuf[d, :, at] = e
-            pbuf[d, :, at] = e.astype(BF)
+            e = jnp.exp2(sbuf[rows, at] * (SCALE * LOG2E) - top_row[:, at])
+            sbuf[rows, at] = e
+            pbuf[rows, at] = e.astype(BF)
             total[:, at] += jnp.sum(e.reshape(TOK // 8, 8, CHUNK), axis=0)
         return carry
 
-    lax.fori_loop(0, blocks, numerators, 0)
+    lax.fori_loop(0, BLOCKS, numerators, 0)
     inv = 1.0 / jnp.sum(total[...], axis=0, keepdims=True)
     inv_col = jnp.broadcast_to(inv, (HD, LANES)).T
     gnorm[...] = (gall[...].astype(F32) * inv_col).astype(BF)
 
-    def up(a, r, j):
-        z = zat(j)
+    def up(a, d):
+        r = jnp.where(d <= zh, 0, jnp.where(d <= zh + NZ, 1, 2))
         return remote(
-            part.at[a, r, z], from_x.at[a, r - 1, z], xs.at[a, 4 * (r - 1) + j],
-            xr.at[a, 4 * (r - 1) + j], xdev(NX - r),
+            part.at[a, d], from_x.at[a, d], xs.at[a, d], xr.at[a, d],
+            {"context": lax.rem(c - NZ * r + NX * NZ, NX * NZ)},
         )
 
-    def up_all(a, act):
-        for j in range(NZ):
-            @pl.when(x > 0)
+    def up_if(a, d, act):
+        if d:
+            @pl.when((d > zh) & (d <= c))
             def _():
-                act(up(a, 1, j))
-
-            @pl.when((x > 1) & (zat(j) >= zh))
-            def _():
-                act(up(a, 2, j))
+                act(up(a, d))
+
+    def from_below(a, d):
+        remote(part.at[a, d], from_x.at[a, d], xs.at[a, d], xr.at[a, d], xdev(1)).wait_recv()
+        acc[...] += from_x[a, d].astype(F32)
 
     def over(a, j):
         return remote(zsend.at[a, zat(j)], from_z.at[a, j], zs.at[a, j], zr.at[a, j], zdev(j))
@@ -275,57 +250,51 @@
     def sum_rows(a):
         for j in (2, 1, 3, 0):
             z = zat(j)
-            acc[...] = part[a, 0, z].astype(F32)
+            d = zh - z
+
+            @pl.when(d >= 0)
+            def _():
+                acc[...] = part[a, d].astype(F32)
+
+            @pl.when(d < 0)
+            def _():
+                acc[...] = jnp.zeros((TOK, HD), F32)
 
             @pl.when(x < NX - 1)
             def _():
-                up(a, 1, j).wait_recv()
-                acc[...] += from_x[a, 0, z].astype(F32)
-
-            @pl.when((x < NX - 2) & (z >= zh))
+                from_below(a, NZ + d)
+
+            @pl.when((x < NX - 2) & (d <= 0))
             def _():
-                up(a, 2, j).wait_recv()
-                acc[...] += from_x[a, 1, z].astype(F32)
+                from_below(a, 2 * NZ + d)
 
             if j:
                 zsend[a, z] = acc[...].astype(BF)
                 over(a, j).start()
             else:
-                part[a, 0, z] = acc[...].astype(BF)
+                zown[a] = acc[...]
 
     def sum_ring(a):
-        out = part[a, 0, zh].astype(F32)
+        out = zown[a]
         for j in (1, 3, 2):
             over(a, j).wait_recv()
             out = out + from_z[a, j].astype(F32)
         return out.astype(BF)
 
-    def value_parts(r):
-        def step(j, carry):
-            z = zat(j)
-
-            @pl.when(there(r, j))
-            def _():
-                part[1, r, z] = dot(pbuf[NZ * r + zh - z], gnorm[...]).astype(BF)
-                if r:
-                    up(1, r, j).start()
-
-            return carry
-
-        return step
-
-    for r in (2, 1, 0):
-        lax.fori_loop(0, NZ, value_parts(r), 0)
-
-    from_above(1)
-    ot[...] = jnp.zeros((HD, LANES), F32)
-
-    def attend(d, carry):
-        r, z = slot(d)
-        ot[...] += dot(kv[1, r, z].T, pbuf[d])
-        return carry
-
-    lax.fori_loop(0, blocks, attend, 0)
+    def group_rows(g):
+        return slice(GROUP * TOK * g, GROUP * TOK * (g + 1))
+
+    def put_parts(a, g, product):
+        part[a, GROUP * g : GROUP * (g + 1)] = product.astype(BF).reshape(GROUP, TOK, HD)
+        for d in reversed(range(GROUP * g, GROUP * (g + 1))):
+            up_if(a, d, start)
+
+    for g in (2, 1, 0):
+        put_parts(1, g, dot(pbuf[group_rows(g), :], gnorm[...]))
+
+    for d in range(1, BLOCKS):
+        from_above(1, d)
+    ot[...] = dot_rows(kv[1, :BLOCKS].reshape(BLOCKS * TOK, HD), pbuf[...])
     att = (ot[...] * inv).astype(BF).astype(F32)
     delta = jnp.sum(att * gt[...].astype(F32), axis=0, keepdims=True)
     att_rows = att.T.astype(BF)
@@ -336,35 +305,20 @@
 
     sum_rows(1)
 
-    dqt[...] = jnp.zeros((HD, LANES), F32)
     inv_scaled = inv * SCALE
 
-    def grads(r, j):
-        z = zat(j)
-        d = NZ * r + zh - z
-        vb = kv[1, r, z]
-        kt = kv[0, r, z].T
+    def grads(g):
+        vb = kv[1, GROUP * g : GROUP * (g + 1)].reshape(GROUP * TOK, HD)
+        rows = group_rows(g)
         for i in range(LANES // CHUNK):
             at = slice(CHUNK * i, CHUNK * (i + 1))
             dprob = dot(vb, gt[:, at])
-            pbuf[d, :, at] = (sbuf[d, :, at] * ((dprob - delta[:, at]) * inv_scaled[:, at])).astype(BF)
-        part[0, r, z] = dot(pbuf[d], qall[...]).astype(BF)
-        dqt[...] += dot(kt, pbuf[d])
-
-    def grad_parts(r):
-        def step(j, carry):
-            @pl.when(there(r, j))
-            def _():
-                grads(r, j)
-                if r:
-                    up(0, r, j).start()
-
-            return carry
-
-        return step
-
-    for r in (2, 1, 0):
-        lax.fori_loop(0, NZ, grad_parts(r), 0)
+            pbuf[rows, at] = (sbuf[rows, at] * ((dprob - delta[:, at]) * inv_scaled[:, at])).astype(BF)
+        put_parts(0, g, dot(pbuf[rows, :], qall[...]))
+
+    for g in (2, 1, 0):
+        grads(g)
+    dqt[...] = dot_rows(kv[0, :BLOCKS].reshape(BLOCKS * TOK, HD), pbuf[...])
     dq_rows = dqt[...].T.astype(BF)
     for h in range(HEADS):
         grad_rows[:, HD * h : HD * (h + 1)] = dq_rows[TOK * h : TOK * (h + 1), :]
@@ -429,7 +383,8 @@
             ring(a, i).wait_send()
         for j in range(NZ):
             down_all(a, j, wait_send)
-        up_all(a, wait_send)
+        for d in range(1, BLOCKS):
+            up_if(a, d, wait_send)
         for j in range(1, NZ):
             over(a, j).wait_send()
     for k in range(NDP):
@@ -476,24 +431,25 @@
             vmem((TOK, D), BF),
             vmem((D, HD), BF),
             vmem((1, SEQ), jnp.int32),
-            vmem((2, 3, NZ, TOK, HD), BF),
+            vmem((2, SLOTS, TOK, HD), BF),
             vmem((LANES, HD), BF),
             vmem((LANES, HD), BF),
             vmem((LANES, HD), BF),
             vmem((HD, LANES), BF),
             vmem((HD, LANES), BF),
             vmem((D, TOK), BF),
-            vmem((SPAN + 1, TOK, LANES), F32),
-            vmem((SPAN + 1, TOK, LANES), BF),
+            vmem((BLOCKS * TOK, LANES), F32),
+            vmem((BLOCKS * TOK, LANES), BF),
             vmem((8, LANES), F32),
             vmem((8, LANES), F32),
             vmem((HD, LANES), F32),
             vmem((HD, LANES), F32),
             vmem((TOK, HEADS * HD), BF),
             vmem((TOK, HEADS * HD), BF),
-            vmem((2, 3, NZ, TOK, HD), BF),
-            vmem((2, 2, NZ, TOK, HD), BF),
+            vmem((2, BLOCKS, TOK, HD), BF),
+            vmem((2, BLOCKS, TOK, HD), BF),
             vmem((TOK, HD), F32),
+            vmem((2, TOK, HD), F32),
             vmem((2, NZ, TOK, HD), BF),
             vmem((2, NZ, TOK, HD), BF),
             vmem((TOK, HD), BF),
@@ -508,8 +464,9 @@
             vmem((NZ, ROWS_OUT, HD), BF),
             vmem((ROWS_OUT, HD), F32),
             dma((10,)),
-            dma((2, 12)), dma((2, 12)),
-            dma((2, 8)), dma((2, 8)),
+            dma((2, NZ)), dma((2, NZ)),
+            dma((2, BLOCKS)), dma((2, BLOCKS)),
+            dma((2, BLOCKS)), dma((2, BLOCKS)),
             dma((2, NZ)), dma((2, NZ)),
             dma((NDP, NX)), dma((NDP, NX)),
             dma((NDP,)), dma((NDP,)),

time: 82 us -> 84.6 us (1.032)
  the two profiles are of different devices: /device:TPU:26 before, /device:TPU:2 now
where the time goes in v3:
time: 84.6 us; the launch traced here: 84.5 us
  Pallas kernels  83.8 us (99%)
    pallas_call x1, Pallas kernels, on_device(): pl.pallas_call(kernel, out_shape=(shape((1, TOK, HEADS * HD), BF), shape(...  82 us
    pallas_call x1, Pallas kernels, on_device(): pl.pallas_call(hand_over, out_shape=tuple((shape(o.shape, o.dtype) for o...  1.85 us

profile of v3, /device:TPU:2, one launch (start us, length us, event | category | flops | bytes accessed | tf_op | source)
XLA Modules:
  0.0 84.5 jit_solution(7206669770726368490)
XLA Ops:
  0.6 82.0 %cross_attention.1 = (bf16[1,192,640]{2,1,0:T(8,128)(2,1)}, bf16[1,192,640]{2,1,0:T(8,128)(2,1)}, bf16[1,192,128]{2,1,0:T(8,128)(2,1)}, f32[80,128]{1,0:T(8,128)}) custom-call(bf16[1,192,640]{2,1,0:T(8,128)(2,1)} %q_hbm.1, bf16[1,192,128]{2,1,0:T(8,128)(2,1)} %k_hbm.1, bf16[1,192,5120]{2,1,0:T(8,128)(2,1)} %mem_hbm.1, bf16[5120,128]{1,0:T(8,128)(2,1)} %w_hbm.1, ...), custom_call_target="tpu_custom_call" | custom-call | tf_op jit(solution)/shard_map/cross_attention/pallas_call | solution.py:418
  82.6 1.8 %hand_over.1 = (bf16[1,192,640]{2,1,0:T(8,128)(2,1)}, bf16[1,192,640]{2,1,0:T(8,128)(2,1)}, bf16[1,192,128]{2,1,0:T(8,128)(2,1)}, f32[80,128]{1,0:T(8,128)}) custom-call(bf16[1,192,640]{2,1,0:T(8,128)(2,1)} %get-tuple-element.8.refs_0_, bf16[1,192,640]{2,1,0:T(8,128)(2,1)} %get-tuple-element.9.refs_1_, bf16[1,192,128]{2,1,0:T(8,128)(2,1)} %get-tuple-element.10.refs_2_, ...), custom_call_target="tpu_custom_call" | custom-call | tf_op jit(solution)/shard_map/hand_over/pallas_call | solution.py:480

commit v4 on v3

--- a/solution.py
+++ b/solution.py
@@ -20,14 +20,17 @@
 NX = 4
 NZ = 4
 NDP = 4
+NT = 8
 SPAN = 8
 BLOCKS = SPAN + 1
 SLOTS = BLOCKS + NZ - 1
 GROUP = 3
+SENDS = ((2, 1), (3, 5, 8, 4), (6, 7))
 LANES = 1024
 CHUNK = 256
 ROWS_X = D // (NDP * NX)
 ROWS_OUT = ROWS_X // NZ
+ROWS_T = NDP * ROWS_X // NT
 SCALE = HD ** (-0.5)
 LOG2E = math.log2(math.e)
 NEG = -1e30
@@ -53,12 +56,13 @@
     q_in, g_in, mem, w, doc,
     kv, qall, gall, gnorm, qt, gt, memt,
     sbuf, pbuf, top, total, ot, dqt, out_rows, grad_rows,
-    part, from_x, acc, zown, zsend, from_z, gk_out, dv,
-    wsend, wown, wrecv, dsend, dacc, drecv, hsend, hrecv, gw_out,
-    lsem, cs, cr, gs, gr, xs, xr, zs, zr, ws, wr, ds, dr, hs, hr,
+    part, from_x, acc, zown, zsend, from_z, gk_out, dvx,
+    mq, dsend, dacc, drecv, hsend, hrecv, gw_out,
+    lsem, cs, cr, gs, gr, xs, xr, zs, zr, ms, mr, ns, nr, vs, vr, ds, dr, hs, hr,
 ):
     c = lax.axis_index("context")
     dp = lax.axis_index("dp")
+    t = lax.axis_index("tensor")
     x = c // NZ
     zh = c % NZ
 
@@ -73,6 +77,9 @@
 
     def dpdev(j):
         return {"dp": lax.rem(dp + j, NDP)}
+
+    def tdev(j):
+        return {"tensor": lax.rem(t + j, NT)}
 
     loads = [
         pltpu.make_async_copy(k_hbm.at[0], kv.at[0, 0], lsem.at[0]),
@@ -89,19 +96,40 @@
     for j in range(1, 4):
         for device in (zdev(j), xdev(j), dpdev(j)):
             pl.semaphore_signal(barrier, inc=1, device_id=device, device_id_type=MESH)
+    for j in range(1, NT):
+        pl.semaphore_signal(barrier, inc=1, device_id=tdev(j), device_id_type=MESH)
 
     def slot(z, h):
         e = h - z
         return jnp.where(e < 0, e + SLOTS, e)
 
     def ring(a, i):
-        to = (1, 3)[i % 2]
-        z = (zh, zh, zat(3), zat(1))[i]
-        rows = (pl.ds(0, TOK), pl.ds(0, TOK), pl.ds(0, HALF), pl.ds(HALF, HALF))[i]
+        to = (1, 1, 3, 3, 1, 3)[i]
+        z = (zh, zh, zh, zh, zat(3), zat(1))[i]
+        rows = pl.ds((0, HALF, HALF, 0, 0, HALF)[i], HALF)
         return remote(
             kv.at[a, slot(z, zh), rows], kv.at[a, slot(z, zat(to)), rows],
             cs.at[a, i], cr.at[a, i], zdev(to),
         )
+
+    def ring_start(a):
+        for i in (0, 2, 1, 3):
+            ring(a, i).start()
+
+    def ring_forward(a):
+        ring(a, 0).wait_recv()
+        ring(a, 4).start()
+        ring(a, 2).wait_recv()
+        ring(a, 5).start()
+        ring(a, 1).wait_recv()
+        down_all(a, 3, start)
+        ring(a, 3).wait_recv()
+        down_all(a, 1, start)
+
+    def ring_end(a):
+        ring(a, 4).wait_recv()
+        ring(a, 5).wait_recv()
+        down_all(a, 2, start)
 
     def down(a, r, j):
         z = zat(j)
@@ -130,17 +158,28 @@
         copy.wait_send()
 
     loads[0].wait()
-    pl.semaphore_wait(barrier, 9)
-    ring(0, 0).start()
-    ring(0, 1).start()
+    pl.semaphore_wait(barrier, 9 + NT - 1)
+    ring_start(0)
     down_all(0, 0, start)
 
     loads[1].wait()
     loads[2].wait()
     kv[1, 0] = dot(mem[...], w[...]).astype(BF)
-    ring(1, 0).start()
-    ring(1, 1).start()
+    ring_start(1)
     down_all(1, 0, start)
+
+    def fetch(o):
+        row = NX * ROWS_X * (t // 2) + ROWS_X * lax.rem(x + o, NX) + ROWS_T * (t % 2)
+        return remote(
+            memt.at[pl.ds(pl.multiple_of(row, 16), ROWS_T)], mq.at[o, t], ms.at[o], mr.at[o], xdev(o)
+        )
+
+    def share(o, k):
+        return remote(mq.at[o, t], mq.at[o, t], ns.at[o, k], nr.at[o, k], tdev(k))
+
+    memt[...] = mem[...].T
+    for o in range(1, NX):
+        fetch(o).start()
 
     loads[3].wait()
     loads[4].wait()
@@ -187,25 +226,15 @@
             sbuf[rows, at] = s
             top[:, at] = jnp.maximum(top[:, at], jnp.max(s.reshape(TOK // 8, 8, CHUNK), axis=0))
 
-    ring(0, 0).wait_recv()
-    ring(0, 2).start()
-    ring(0, 1).wait_recv()
-    ring(0, 3).start()
-    down_all(0, 1, start)
-    down_all(0, 3, start)
-    ring(1, 0).wait_recv()
-    ring(1, 2).start()
-    ring(1, 1).wait_recv()
-    ring(1, 3).start()
-    down_all(1, 1, start)
-    down_all(1, 3, start)
-    ring(0, 2).wait_recv()
-    ring(0, 3).wait_recv()
-    down_all(0, 2, start)
+    ring_forward(0)
+    ring_forward(1)
+    ring_end(0)
+    for o in range(1, NX):
+        fetch(o).wait_recv()
+        for k in range(1, NT):
+            share(o, k).start()
     scores(0)
-    ring(1, 2).wait_recv()
-    ring(1, 3).wait_recv()
-    down_all(1, 2, start)
+    ring_end(1)
     for d in (4, 8, 1, 3, 5, 7, 2, 6):
         from_above(0, d)
         scores(d)
@@ -286,10 +315,10 @@
 
     def put_parts(a, g, product):
         part[a, GROUP * g : GROUP * (g + 1)] = product.astype(BF).reshape(GROUP, TOK, HD)
-        for d in reversed(range(GROUP * g, GROUP * (g + 1))):
+        for d in SENDS[g]:
             up_if(a, d, start)
 
-    for g in (2, 1, 0):
+    for g in (2, 0, 1):
         put_parts(1, g, dot(pbuf[group_rows(g), :], gnorm[...]))
 
     for d in range(1, BLOCKS):
@@ -316,7 +345,7 @@
             pbuf[rows, at] = (sbuf[rows, at] * ((dprob - delta[:, at]) * inv_scaled[:, at])).astype(BF)
         put_parts(0, g, dot(pbuf[rows, :], qall[...]))
 
-    for g in (2, 1, 0):
+    for g in (2, 0, 1):
         grads(g)
     dqt[...] = dot_rows(kv[0, :BLOCKS].reshape(BLOCKS * TOK, HD), pbuf[...])
     dq_rows = dqt[...].T.astype(BF)
@@ -325,11 +354,8 @@
     store_gq = pltpu.make_async_copy(grad_rows, gq_hbm.at[0], lsem.at[7])
     store_gq.start()
 
-    memt[...] = mem[...].T
-    dv[...] = sum_ring(1)
-
-    def wx(k, o):
-        return remote(wsend.at[k, o], wrecv.at[k, o], ws.at[k, o], wr.at[k, o], xdev(o))
+    def spread(o):
+        return remote(dvx.at[0], dvx.at[o], vs.at[o], vr.at[o], xdev(o))
 
     def wd(k):
         return remote(dsend.at[k], drecv.at[k], ds.at[k], dr.at[k], dpdev(k + 1))
@@ -337,23 +363,23 @@
     def wh(o):
         return remote(hsend.at[o], hrecv.at[o], hs.at[o], hr.at[o], zdev(o))
 
+    dvx[0] = sum_ring(1)
+    for o in range(1, NX):
+        spread(o).start()
+    sum_rows(0)
+
+    for o in range(1, NX):
+        for k in range(1, NT):
+            share(o, k).wait_recv()
+    for o in range(1, NX):
+        spread(o).wait_recv()
     for k in range(NDP):
-        for o in (2, 1, 3, 0):
-            row = NX * ROWS_X * lax.rem(dp + 1 + k, NDP) + ROWS_X * lax.rem(x + o, NX)
-            piece = dot(memt[pl.ds(pl.multiple_of(row, 64), ROWS_X), :], dv[...])
-            if o:
-                wsend[k, o] = piece.astype(BF)
-                wx(k, o).start()
-            else:
-                wown[k] = piece
-
-    sum_rows(0)
-
-    for k in range(NDP):
-        piece = wown[k]
-        for o in (1, 3, 2):
-            wx(k, o).wait_recv()
-            piece = piece + wrecv[k, o].astype(F32)
+        to = lax.rem(dp + 1 + k, NDP)
+        row = NX * ROWS_X * to + ROWS_X * x
+        piece = dot(memt[pl.ds(pl.multiple_of(row, 64), ROWS_X), :], dvx[0])
+        for o in range(1, NX):
+            own = mq[o, pl.ds(2 * to, 2)].reshape(ROWS_X, TOK)
+            piece = piece + dot(own, dvx[o])
         if k < NDP - 1:
             dsend[k] = piece.astype(BF)
             wd(k).start()
@@ -379,7 +405,7 @@
     store_gw.start()
 
     for a in range(2):
-        for i in range(4):
+        for i in range(6):
             ring(a, i).wait_send()
         for j in range(NZ):
             down_all(a, j, wait_send)
@@ -387,9 +413,11 @@
             up_if(a, d, wait_send)
         for j in range(1, NZ):
             over(a, j).wait_send()
-    for k in range(NDP):
-        for o in range(1, NX):
-            wx(k, o).wait_send()
+    for o in range(1, NX):
+        fetch(o).wait_send()
+        spread(o).wait_send()
+        for k in range(1, NT):
+            share(o, k).wait_send()
     for k in range(NDP - 1):
         wd(k).wait_send()
     for o in range(1, NZ):
@@ -453,10 +481,8 @@
             vmem((2, NZ, TOK, HD), BF),
             vmem((2, NZ, TOK, HD), BF),
             vmem((TOK, HD), BF),
-            vmem((TOK, HD), BF),
-            vmem((NDP, NX, ROWS_X, HD), BF),
-            vmem((NDP, ROWS_X, HD), F32),
-            vmem((NDP, NX, ROWS_X, HD), BF),
+            vmem((NX, TOK, HD), BF),
+            vmem((NX, NT, ROWS_T, TOK), BF),
             vmem((NDP, ROWS_X, HD), BF),
             vmem((ROWS_X, HD), F32),
             vmem((NDP, ROWS_X, HD), BF),
@@ -464,11 +490,13 @@
             vmem((NZ, ROWS_OUT, HD), BF),
             vmem((ROWS_OUT, HD), F32),
             dma((10,)),
-            dma((2, NZ)), dma((2, NZ)),
+            dma((2, 6)), dma((2, 6)),
             dma((2, BLOCKS)), dma((2, BLOCKS)),
             dma((2, BLOCKS)), dma((2, BLOCKS)),
             dma((2, NZ)), dma((2, NZ)),
-            dma((NDP, NX)), dma((NDP, NX)),
+            dma((NX,)), dma((NX,)),
+            dma((NX, NT)), dma((NX, NT)),
+            dma((NX,)), dma((NX,)),
             dma((NDP,)), dma((NDP,)),
             dma((NZ,)), dma((NZ,)),
         ],

time: 84.6 us -> 79.6 us (0.941)
  the two profiles are of different devices: /device:TPU:2 before, /device:TPU:16 now
where the time goes in v4:
time: 79.6 us; the launch traced here: 79.5 us
  Pallas kernels  78.8 us (99%)
    pallas_call x1, Pallas kernels, on_device(): pl.pallas_call(kernel, out_shape=(shape((1, TOK, HEADS * HD), BF), shape(...  77 us
    pallas_call x1, Pallas kernels, on_device(): pl.pallas_call(hand_over, out_shape=tuple((shape(o.shape, o.dtype) for o...  1.85 us

profile of v4, /device:TPU:16, one launch (start us, length us, event | category | flops | bytes accessed | tf_op | source)
XLA Modules:
  0.0 79.5 jit_solution(14479183758351573894)
XLA Ops:
  0.6 77.0 %cross_attention.1 = (bf16[1,192,640]{2,1,0:T(8,128)(2,1)}, bf16[1,192,640]{2,1,0:T(8,128)(2,1)}, bf16[1,192,128]{2,1,0:T(8,128)(2,1)}, f32[80,128]{1,0:T(8,128)}) custom-call(bf16[1,192,640]{2,1,0:T(8,128)(2,1)} %q_hbm.1, bf16[1,192,128]{2,1,0:T(8,128)(2,1)} %k_hbm.1, bf16[1,192,5120]{2,1,0:T(8,128)(2,1)} %mem_hbm.1, bf16[5120,128]{1,0:T(8,128)(2,1)} %w_hbm.1, ...), custom_call_target="tpu_custom_call" | custom-call | tf_op jit(solution)/shard_map/cross_attention/pallas_call | solution.py:446
  77.6 1.8 %hand_over.1 = (bf16[1,192,640]{2,1,0:T(8,128)(2,1)}, bf16[1,192,640]{2,1,0:T(8,128)(2,1)}, bf16[1,192,128]{2,1,0:T(8,128)(2,1)}, f32[80,128]{1,0:T(8,128)}) custom-call(bf16[1,192,640]{2,1,0:T(8,128)(2,1)} %get-tuple-element.8.refs_0_, bf16[1,192,640]{2,1,0:T(8,128)(2,1)} %get-tuple-element.9.refs_1_, bf16[1,192,128]{2,1,0:T(8,128)(2,1)} %get-tuple-element.10.refs_2_, ...), custom_call_target="tpu_custom_call" | custom-call | tf_op jit(solution)/shard_map/hand_over/pallas_call | solution.py:508

commit v5 on v4

--- a/solution.py
+++ b/solution.py
@@ -21,6 +21,8 @@
 NZ = 4
 NDP = 4
 NT = 8
+NRING = NDP * NZ
+RELAYS = (2, -2, 6, -6)
 SPAN = 8
 BLOCKS = SPAN + 1
 SLOTS = BLOCKS + NZ - 1
@@ -57,7 +59,7 @@
     kv, qall, gall, gnorm, qt, gt, memt,
     sbuf, pbuf, top, total, ot, dqt, out_rows, grad_rows,
     part, from_x, acc, zown, zsend, from_z, gk_out, dvx,
-    mq, dsend, dacc, drecv, hsend, hrecv, gw_out,
+    mq, wacc, dsend, drecv, hsend, hrecv,
     lsem, cs, cr, gs, gr, xs, xr, zs, zr, ms, mr, ns, nr, vs, vr, ds, dr, hs, hr,
 ):
     c = lax.axis_index("context")
@@ -75,8 +77,14 @@
     def xdev(j):
         return {"context": lax.rem(c + NZ * j, NX * NZ)}
 
-    def dpdev(j):
-        return {"dp": lax.rem(dp + j, NDP)}
+    p = NDP * zh + dp
+
+    def along(o):
+        return lax.rem(p + o + NRING, NRING)
+
+    def pdev(o):
+        to = along(o)
+        return {"dp": lax.rem(to, NDP), "context": x * NZ + to // NDP}
 
     def tdev(j):
         return {"tensor": lax.rem(t + j, NT)}
@@ -94,8 +102,10 @@
 
     barrier = pltpu.get_barrier_semaphore()
     for j in range(1, 4):
-        for device in (zdev(j), xdev(j), dpdev(j)):
+        for device in (zdev(j), xdev(j)):
             pl.semaphore_signal(barrier, inc=1, device_id=device, device_id_type=MESH)
+    for o in (1, -1) + RELAYS:
+        pl.semaphore_signal(barrier, inc=1, device_id=pdev(o), device_id_type=MESH)
     for j in range(1, NT):
         pl.semaphore_signal(barrier, inc=1, device_id=tdev(j), device_id_type=MESH)
 
@@ -158,7 +168,7 @@
         copy.wait_send()
 
     loads[0].wait()
-    pl.semaphore_wait(barrier, 9 + NT - 1)
+    pl.semaphore_wait(barrier, 6 + 6 + NT - 1)
     ring_start(0)
     down_all(0, 0, start)
 
@@ -321,6 +331,8 @@
     for g in (2, 0, 1):
         put_parts(1, g, dot(pbuf[group_rows(g), :], gnorm[...]))
 
+    sum_rows(1)
+
     for d in range(1, BLOCKS):
         from_above(1, d)
     ot[...] = dot_rows(kv[1, :BLOCKS].reshape(BLOCKS * TOK, HD), pbuf[...])
@@ -332,8 +344,6 @@
     store_att = pltpu.make_async_copy(out_rows, att_hbm.at[0], lsem.at[6])
     store_att.start()
 
-    sum_rows(1)
-
     inv_scaled = inv * SCALE
 
     def grads(g):
@@ -357,11 +367,19 @@
     def spread(o):
         return remote(dvx.at[0], dvx.at[o], vs.at[o], vr.at[o], xdev(o))
 
-    def wd(k):
-        return remote(dsend.at[k], drecv.at[k], ds.at[k], dr.at[k], dpdev(k + 1))
-
-    def wh(o):
-        return remote(hsend.at[o], hrecv.at[o], hs.at[o], hr.at[o], zdev(o))
+    side = 1 - 2 * lax.rem(t, 2)
+    near = (-2 * side, side, -side)
+
+    def wd(i):
+        return remote(dsend.at[i], drecv.at[i], ds.at[i], dr.at[i], pdev(near[i]))
+
+    def wh(i):
+        return remote(hsend.at[i], hrecv.at[i], hs.at[i], hr.at[i], pdev(RELAYS[i]))
+
+    def rows_of(o):
+        to = along(o)
+        row = ROWS_X * lax.rem(to, NDP) + ROWS_OUT * (to // NDP)
+        return pl.ds(pl.multiple_of(row, 16), ROWS_OUT)
 
     dvx[0] = sum_ring(1)
     for o in range(1, NX):
@@ -374,35 +392,33 @@
     for o in range(1, NX):
         spread(o).wait_recv()
     for k in range(NDP):
-        to = lax.rem(dp + 1 + k, NDP)
-        row = NX * ROWS_X * to + ROWS_X * x
+        rows = slice(ROWS_X * k, ROWS_X * (k + 1))
+        row = NX * ROWS_X * k + ROWS_X * x
         piece = dot(memt[pl.ds(pl.multiple_of(row, 64), ROWS_X), :], dvx[0])
         for o in range(1, NX):
-            own = mq[o, pl.ds(2 * to, 2)].reshape(ROWS_X, TOK)
-            piece = piece + dot(own, dvx[o])
-        if k < NDP - 1:
-            dsend[k] = piece.astype(BF)
-            wd(k).start()
-        else:
-            dacc[...] = piece
-    for k in range(NDP - 1):
-        wd(k).wait_recv()
-        dacc[...] += drecv[k].astype(F32)
-    for o in (2, 1, 3):
-        rows = pl.ds(pl.multiple_of(ROWS_OUT * zat(o), 16), ROWS_OUT)
-        hsend[o] = dacc[rows, :].astype(BF)
-        wh(o).start()
+            piece = piece + dot(mq[o, 2 * k : 2 * k + 2].reshape(ROWS_X, TOK), dvx[o])
+        wacc[rows, :] = piece
+    for i in range(3):
+        for e in range(4):
+            dsend[i, e] = wacc[rows_of(near[i] + RELAYS[e]), :].astype(BF)
+        wd(i).start()
+    for i in range(3):
+        wd(i).wait_recv()
+    for e in (2, 3, 0, 1):
+        piece = wacc[rows_of(RELAYS[e]), :]
+        for i in range(3):
+            piece = piece + drecv[i, e].astype(F32)
+        hsend[e] = piece.astype(BF)
+        wh(e).start()
     gk_out[...] = sum_ring(0)
     store_gk = pltpu.make_async_copy(gk_out, gk_hbm.at[0], lsem.at[8])
     store_gk.start()
 
-    out = dacc[pl.ds(pl.multiple_of(ROWS_OUT * zh, 16), ROWS_OUT), :]
-    for o in (1, 3, 2):
-        wh(o).wait_recv()
-        out = out + hrecv[o].astype(F32)
-    gw_out[...] = out
-    store_gw = pltpu.make_async_copy(gw_out, gw_hbm, lsem.at[9])
-    store_gw.start()
+    out = jnp.zeros((ROWS_OUT, HD), F32)
+    for e in range(4):
+        wh(e).wait_recv()
+        out = out + hrecv[e].astype(F32)
+    gw_hbm[...] = out
 
     for a in range(2):
         for i in range(6):
@@ -418,23 +434,19 @@
         spread(o).wait_send()
         for k in range(1, NT):
             share(o, k).wait_send()
-    for k in range(NDP - 1):
-        wd(k).wait_send()
-    for o in range(1, NZ):
-        wh(o).wait_send()
-    for store in (store_att, store_gq, store_gk, store_gw):
+    for i in range(3):
+        wd(i).wait_send()
+    for e in range(4):
+        wh(e).wait_send()
+    for store in (store_att, store_gq, store_gk):
         store.wait()
 
 
 def hand_over(*refs):
-    into = [pltpu.make_async_copy(refs[i], refs[8 + i], refs[12].at[i]) for i in range(4)]
-    back = [pltpu.make_async_copy(refs[8 + i], refs[4 + i], refs[13].at[i]) for i in range(4)]
-    for copy in into:
+    copies = [pltpu.make_async_copy(refs[i], refs[4 + i], refs[8].at[i]) for i in range(4)]
+    for copy in copies:
         copy.start()
-    for i in range(4):
-        into[i].wait()
-        back[i].start()
-    for copy in back:
+    for copy in copies:
         copy.wait()
 
 
@@ -452,7 +464,7 @@
             shape((ROWS_OUT, HD), F32),
         ),
         in_specs=[pl.BlockSpec(memory_space=pltpu.HBM)] * 6,
-        out_specs=(anywhere,) * 4,
+        out_specs=(pl.BlockSpec(memory_space=pltpu.VMEM),) * 4,
         scratch_shapes=[
             vmem((TOK, HEADS * HD), BF),
             vmem((TOK, HEADS * HD), BF),
@@ -483,12 +495,11 @@
             vmem((TOK, HD), BF),
             vmem((NX, TOK, HD), BF),
             vmem((NX, NT, ROWS_T, TOK), BF),
-            vmem((NDP, ROWS_X, HD), BF),
-            vmem((ROWS_X, HD), F32),
-            vmem((NDP, ROWS_X, HD), BF),
-            vmem((NZ, ROWS_OUT, HD), BF),
-            vmem((NZ, ROWS_OUT, HD), BF),
-            vmem((ROWS_OUT, HD), F32),
+            vmem((NDP * ROWS_X, HD), F32),
+            vmem((3, 4, ROWS_OUT, HD), BF),
+            vmem((3, 4, ROWS_OUT, HD), BF),
+            vmem((4, ROWS_OUT, HD), BF),
+            vmem((4, ROWS_OUT, HD), BF),
             dma((10,)),
             dma((2, 6)), dma((2, 6)),
             dma((2, BLOCKS)), dma((2, BLOCKS)),
@@ -497,8 +508,8 @@
             dma((NX,)), dma((NX,)),
             dma((NX, NT)), dma((NX, NT)),
             dma((NX,)), dma((NX,)),
-            dma((NDP,)), dma((NDP,)),
-            dma((NZ,)), dma((NZ,)),
+            dma((3,)), dma((3,)),
+            dma((4,)), dma((4,)),
         ],
         compiler_params=pltpu.CompilerParams(
             collective_id=0, has_side_effects=True, vmem_limit_bytes=60 << 20
@@ -508,9 +519,9 @@
     return pl.pallas_call(
         hand_over,
         out_shape=tuple(shape(o.shape, o.dtype) for o in outs),
-        in_specs=[anywhere] * 4,
+        in_specs=[pl.BlockSpec(memory_space=pltpu.VMEM)] * 4,
         out_specs=(anywhere,) * 4,
-        scratch_shapes=[*(vmem(o.shape, o.dtype) for o in outs), dma((4,)), dma((4,))],
+        scratch_shapes=[dma((4,))],
         compiler_params=pltpu.CompilerParams(vmem_limit_bytes=60 << 20),
         name="hand_over",
     )(*outs)

time: 79.6 us -> 79.1 us (level)
  the two profiles are of different devices: /device:TPU:16 before, /device:TPU:40 now
where the time goes in v5:
time: 79.1 us; the launch traced here: 79 us
  Pallas kernels  78.3 us (99%)
    pallas_call x1, Pallas kernels, on_device(): pl.pallas_call(kernel, out_shape=(shape((1, TOK, HEADS * HD), BF), shape(...  76.4 us
    pallas_call x1, Pallas kernels, on_device(): pl.pallas_call(hand_over, out_shape=tuple((shape(o.shape, o.dtype) for o...  1.9 us

profile of v5, /device:TPU:40, one launch (start us, length us, event | category | flops | bytes accessed | tf_op | source)
XLA Modules:
  0.0 79.0 jit_solution(18046935424825717494)
XLA Ops:
  0.6 76.4 %cross_attention.1 = (bf16[1,192,640]{2,1,0:T(8,128)(2,1)}, bf16[1,192,640]{2,1,0:T(8,128)(2,1)}, bf16[1,192,128]{2,1,0:T(8,128)(2,1)}, f32[80,128]{1,0:T(8,128)}) custom-call(bf16[1,192,640]{2,1,0:T(8,128)(2,1)} %q_hbm.1, bf16[1,192,128]{2,1,0:T(8,128)(2,1)} %k_hbm.1, bf16[1,192,5120]{2,1,0:T(8,128)(2,1)} %mem_hbm.1, bf16[5120,128]{1,0:T(8,128)(2,1)} %w_hbm.1, ...), custom_call_target="tpu_custom_call" | custom-call | tf_op jit(solution)/shard_map/cross_attention/pallas_call | solution.py:458
  77.1 1.9 %hand_over.1 = (bf16[1,192,640]{2,1,0:T(8,128)(2,1)}, bf16[1,192,640]{2,1,0:T(8,128)(2,1)}, bf16[1,192,128]{2,1,0:T(8,128)(2,1)}, f32[80,128]{1,0:T(8,128)}) custom-call(bf16[1,192,640]{2,1,0:T(8,128)(2,1)} %get-tuple-element.8.refs_0_, bf16[1,192,640]{2,1,0:T(8,128)(2,1)} %get-tuple-element.9.refs_1_, bf16[1,192,128]{2,1,0:T(8,128)(2,1)} %get-tuple-element.10.refs_2_, ...), custom_call_target="tpu_custom_call" | custom-call | tf_op jit(solution)/shard_map/hand_over/pallas_call | solution.py:519

commit v6 on v5

--- a/solution.py
+++ b/solution.py
@@ -357,35 +357,35 @@
 
     for g in (2, 0, 1):
         grads(g)
+
+    def spread(o):
+        return remote(dvx.at[0], dvx.at[o], vs.at[o], vr.at[o], xdev(o))
+
+    side = 1 - 2 * lax.rem(t, 2)
+    near = (-2 * side, side, -side)
+
+    def wd(i):
+        return remote(dsend.at[i], drecv.at[i], ds.at[i], dr.at[i], pdev(near[i]))
+
+    def wh(i):
+        return remote(hsend.at[i], hrecv.at[i], hs.at[i], hr.at[i], pdev(RELAYS[i]))
+
+    def rows_of(o):
+        to = along(o)
+        row = ROWS_X * lax.rem(to, NDP) + ROWS_OUT * (to // NDP)
+        return pl.ds(pl.multiple_of(row, 16), ROWS_OUT)
+
+    dvx[0] = sum_ring(1)
+    for o in range(1, NX):
+        spread(o).start()
+    sum_rows(0)
+
     dqt[...] = dot_rows(kv[0, :BLOCKS].reshape(BLOCKS * TOK, HD), pbuf[...])
     dq_rows = dqt[...].T.astype(BF)
     for h in range(HEADS):
         grad_rows[:, HD * h : HD * (h + 1)] = dq_rows[TOK * h : TOK * (h + 1), :]
     store_gq = pltpu.make_async_copy(grad_rows, gq_hbm.at[0], lsem.at[7])
     store_gq.start()
-
-    def spread(o):
-        return remote(dvx.at[0], dvx.at[o], vs.at[o], vr.at[o], xdev(o))
-
-    side = 1 - 2 * lax.rem(t, 2)
-    near = (-2 * side, side, -side)
-
-    def wd(i):
-        return remote(dsend.at[i], drecv.at[i], ds.at[i], dr.at[i], pdev(near[i]))
-
-    def wh(i):
-        return remote(hsend.at[i], hrecv.at[i], hs.at[i], hr.at[i], pdev(RELAYS[i]))
-
-    def rows_of(o):
-        to = along(o)
-        row = ROWS_X * lax.rem(to, NDP) + ROWS_OUT * (to // NDP)
-        return pl.ds(pl.multiple_of(row, 16), ROWS_OUT)
-
-    dvx[0] = sum_ring(1)
-    for o in range(1, NX):
-        spread(o).start()
-    sum_rows(0)
-
     for o in range(1, NX):
         for k in range(1, NT):
             share(o, k).wait_recv()

time: 79.1 us -> 79.6 us (level)
  no operation moved by 1% of the time
where the time goes in v6:
time: 79.6 us; the launch traced here: 79.4 us
  Pallas kernels  78.8 us (99%)
    pallas_call x1, Pallas kernels, on_device(): pl.pallas_call(kernel, out_shape=(shape((1, TOK, HEADS * HD), BF), shape(...  76.9 us
    pallas_call x1, Pallas kernels, on_device(): pl.pallas_call(hand_over, out_shape=tuple((shape(o.shape, o.dtype) for o...  1.9 us

profile of v6, /device:TPU:40, one launch (start us, length us, event | category | flops | bytes accessed | tf_op | source)
XLA Modules:
  0.0 79.4 jit_solution(9020304391256162377)
XLA Ops:
  0.6 76.9 %cross_attention.1 = (bf16[1,192,640]{2,1,0:T(8,128)(2,1)}, bf16[1,192,640]{2,1,0:T(8,128)(2,1)}, bf16[1,192,128]{2,1,0:T(8,128)(2,1)}, f32[80,128]{1,0:T(8,128)}) custom-call(bf16[1,192,640]{2,1,0:T(8,128)(2,1)} %q_hbm.1, bf16[1,192,128]{2,1,0:T(8,128)(2,1)} %k_hbm.1, bf16[1,192,5120]{2,1,0:T(8,128)(2,1)} %mem_hbm.1, bf16[5120,128]{1,0:T(8,128)(2,1)} %w_hbm.1, ...), custom_call_target="tpu_custom_call" | custom-call | tf_op jit(solution)/shard_map/cross_attention/pallas_call | solution.py:458
  77.5 1.9 %hand_over.1 = (bf16[1,192,640]{2,1,0:T(8,128)(2,1)}, bf16[1,192,640]{2,1,0:T(8,128)(2,1)}, bf16[1,192,128]{2,1,0:T(8,128)(2,1)}, f32[80,128]{1,0:T(8,128)}) custom-call(bf16[1,192,640]{2,1,0:T(8,128)(2,1)} %get-tuple-element.8.refs_0_, bf16[1,192,640]{2,1,0:T(8,128)(2,1)} %get-tuple-element.9.refs_1_, bf16[1,192,128]{2,1,0:T(8,128)(2,1)} %get-tuple-element.10.refs_2_, ...), custom_call_target="tpu_custom_call" | custom-call | tf_op jit(solution)/shard_map/hand_over/pallas_call | solution.py:519
